TPU v7x, 768 devices: a whole 4x8x12 slice. The times are simulated.
768 devices in a mesh: fsdp: 96 (over z, x, core), tp: 8 (over y).
Axes of the slice: x: 4, y: 8, z: 12, core: 2. Of those that a mesh axis runs over, the one named last changes fastest.
Arguments:
- tokens: bfloat16 [12288, 3584], P('fsdp'), may hold values from -6 to 6
- cotangent: bfloat16 [12288, 14336], P('fsdp', 'tp'), may hold values from -6 to 6
- w_blocks: bfloat16 [96, 8, 3, 128, 128], P('fsdp', 'tp'), may hold values from -0.125 to 0.125
- blk_rows: int32 [96, 8, 3], P('fsdp', 'tp'), may hold values from 0 to 27, as said below
- blk_cols: int32 [96, 8, 3], P('fsdp', 'tp'), may hold values from 0 to 13, as said below
- counts: int32 [96, 8], P('fsdp', 'tp'), may hold values from 1 to 3, as said below
Outputs:
- hidden: bfloat16 [12288, 14336], P('fsdp', 'tp')
- input_grad: bfloat16 [12288, 3584], P('fsdp', 'tp')
Inputs may be any that keep to these rules, and one draw needn't show every extreme that they name: `blk_rows`: within one column shard t no two slots, live or not, name the same block. `blk_cols`: block columns within the shard, see blk_rows. `counts`: in every column shard some owner has all 3 slots live.
All inputs are finite; a program needn't handle non-finite values.
Results may differ from a plain program's by a relative error of at most 0.017.
Values may be sent and summed in bfloat16 or wider, within the bound.
No kernel may reach another device: no remote copies, remote signals or barrier semaphores. Data moves between devices by JAX's collectives and lax.ppermute only.
A program may use at most 128 MiB of HBM per device.

v0:
```python
import math

import jax
import jax.numpy as jnp
from jax import lax
from jax.sharding import PartitionSpec as P

gelu_scale = math.sqrt(2.0 / math.pi)


def gelu_parts(preact):
    cube = preact * preact * preact
    tangent = jnp.tanh(gelu_scale * (preact + 0.044715 * cube))
    activated = 0.5 * preact * (1.0 + tangent)
    derivative = 0.5 * (1.0 + tangent) + 0.5 * preact * (1.0 - tangent * tangent) * gelu_scale * (
        1.0 + 3.0 * 0.044715 * preact * preact
    )
    return (activated, derivative)


def per_device(tokens, cotangent, w_blocks, blk_rows, blk_cols, counts):
    block = w_blocks.shape[-1]
    gathered = (
        lax.all_gather(w_blocks, "fsdp", axis=0, tiled=True),
        lax.all_gather(blk_rows, "fsdp", axis=0, tiled=True),
        lax.all_gather(blk_cols, "fsdp", axis=0, tiled=True),
        lax.all_gather(counts, "fsdp", axis=0, tiled=True),
    )
    blocks, rows_all, cols_all, count_all = gathered
    owners = rows_all.shape[0]
    capacity = rows_all.shape[2]
    slot_total = owners * capacity
    live_slot = (jnp.arange(capacity, dtype=jnp.int32)[None, :] < count_all).reshape(slot_total)
    masked = jnp.where(
        live_slot[:, None, None],
        blocks.reshape(slot_total, block, block),
        jnp.zeros((slot_total, block, block), jnp.bfloat16),
    )
    row_index = rows_all.reshape(slot_total)
    col_index = cols_all.reshape(slot_total)
    model_width = tokens.shape[1]
    row_blocks = model_width // block
    col_blocks = cotangent.shape[1] // block
    dense_tile = (
        jnp.zeros((row_blocks, col_blocks, block, block), jnp.bfloat16)
        .at[row_index, col_index]
        .set(masked)
    )
    dense_tile = dense_tile.transpose(0, 2, 1, 3).reshape(model_width, col_blocks * block)
    preact = jnp.dot(tokens, dense_tile, preferred_element_type=jnp.float32)
    activated, derivative = gelu_parts(preact)
    dpre = (cotangent.astype(jnp.float32) * derivative).astype(jnp.bfloat16)
    partial_value = lax.dot_general(
        dpre, dense_tile, (((1,), (1,)), ((), ())), preferred_element_type=jnp.float32
    )
    summed = lax.psum_scatter(
        partial_value.astype(jnp.bfloat16), "tp", scatter_dimension=1, tiled=True
    )
    return (activated.astype(jnp.bfloat16), summed)


def solution(mesh):
    return jax.shard_map(
        per_device,
        mesh=mesh,
        in_specs=(
            P("fsdp", None),
            P("fsdp", "tp"),
            P("fsdp", "tp", None, None, None),
            P("fsdp", "tp", None),
            P("fsdp", "tp", None),
            P("fsdp", "tp"),
        ),
        out_specs=(P("fsdp", "tp"), P("fsdp", "tp")),
        check_vma=False,
    )
```

profile of v0, /device:TPU:1, one launch (start us, length us, event | category | flops | bytes accessed | tf_op | source)
XLA Modules:
  0.0 448.3 jit_solution(15438076295985862001)
XLA Ops:
  7.2 0.0 copy-start
  7.2 0.0 all-gather.2.cloned.1.call-start
  7.2 0.7 all-gather.2.cloned.1.call-update
  7.9 0.0 reduce-scatter.2.cloned.1.call-start
  8.0 67.6 %all_gather.12 = s32[96,1,3]{2,1,0:T(1,128)S(1)} all-gather(s32[1,1,3]{2,1,0:T(1,128)} %param.9), channel_id=1, replica_groups=mesh['fsdp'=96,'tp'=8] {'fsdp'}, dimensions={0}, use_global_device_ids=true | all-gather | bytes 1164 | tf_op jit(solution)/shard_map/all_gather | solution.py:25
  75.5 0.5 broadcast.93
  76.0 0.8 reduce.9
  76.8 0.2 reshape.86
  77.0 55.1 %all_gather.13 = s32[96,1,3]{2,1,0:T(1,128)S(1)} all-gather(s32[1,1,3]{2,1,0:T(1,128)} %param.10), channel_id=1, replica_groups=mesh['fsdp'=96,'tp'=8] {'fsdp'}, dimensions={0}, use_global_device_ids=true | all-gather | bytes 1164 | tf_op jit(solution)/shard_map/all_gather | solution.py:26
  132.1 0.8 reduce.8
  132.9 0.2 reshape.87
  133.7 1.3 dynamic-slice
  135.0 0.7 bitcast_dynamic-update-slice_fusion
  135.6 185.0 %all-reduce = s32[96]{0:T(128)S(1)} all-reduce(s32[96]{0:T(128)S(1)} %bitcast_dynamic-update-slice_fusion), channel_id=1, replica_groups=mesh['fsdp'=96,'tp'=8] {'fsdp'}, use_global_device_ids=true, to_apply=%add | all-reduce | flops 96 | bytes 768
  320.6 0.1 iota_compare_fusion
  320.7 0.2 lt.48
  320.9 1.3 copy.17
  322.2 0.0 all-gather.2.cloned.1.call-done
  322.2 8.0 %bitcast_select_fusion = bf16[288,128,128]{2,1,0:T(8,128)(2,1)} fusion(bf16[96,1,3,128,128]{4,3,2,1,0:T(8,128)(2,1)} %all-gather.2.cloned.1.call-done, pred[288]{0:T(512)(128)(4,1)S(1)} %lt.48), kind=kLoop, calls=%fused_computation.7 | loop fusion | flops 4718592 | bytes 18874656 | tf_op jit(solution)/shard_map/jit(_where)/select_n | solution.py:34
  330.2 7.9 %broadcast_in_dim.17 = bf16[28,14,128,128]{3,2,1,0:T(8,128)(2,1)} broadcast(bf16[]{:T(256)} %constant.9.clone.1), dimensions={} | broadcast | bytes 12845058 | tf_op jit(solution)/shard_map/broadcast_in_dim | solution.py:45
  338.1 46.1 %scatter_fusion = bf16[28,14,128,128]{3,2,1,0:T(8,128)(2,1)} fusion(bf16[28,14,128,128]{3,2,1,0:T(8,128)(2,1)} %broadcast_in_dim.17, s32[288]{0:T(512)S(1)} %fusion.28, bf16[288,128,128]{2,1,0:T(8,128)(2,1)} %bitcast_select_fusion), kind=kCustom, calls=%fused_computation | custom fusion | bytes 28313856 | tf_op jit(solution)/shard_map/scatter | solution.py:47
  384.1 12.6 %copy.16 = bf16[28,128,14,128]{3,2,1,0:T(8,128)(2,1)S(1)} copy(bf16[28,128,14,128]{3,1,2,0:T(8,128)(2,1)} %bitcast.22) | data formatting | bytes 25690112 | tf_op jit(solution)/shard_map/transpose | solution.py:49
  396.7 0.0 copy-done
  396.7 5.5 %multiply_convert_fusion = (bf16[128,1792]{0,1:T(8,128)(2,1)S(1)}, f32[128,1792]{0,1:T(8,128)S(1)}) fusion(bf16[128,3584]{1,0:T(8,128)(2,1)S(1)} %copy-done, bf16[448,8,14,128]{3,2,1,0:T(8,128)(2,1)S(1)} %bitcast.23), kind=kOutput, calls=%fused_computation.21 | convolution fusion | flops 1646231552 | bytes 15138816 | tf_op jit(solution)/shard_map/dot_general | solution.py:50
  402.2 4.6 %fusion.6 = bf16[128,3584]{0,1:T(8,128)(2,1)} fusion(bf16[448,8,14,128]{3,2,1,0:T(8,128)(2,1)S(1)} %bitcast.24, f32[128,1792]{0,1:T(8,128)S(1)} %get-tuple-element.11, bf16[128,1792]{0,1:T(8,128)(2,1)S(1)} %copy.17), kind=kOutput, calls=%fused_computation.8 | convolution fusion | flops 1649213440 | bytes 15138816 | tf_op jit(solution)/shard_map/dot_general | solution.py:53
  406.8 0.0 reduce-scatter.2.cloned.1.call-update
  406.9 1.0 copy.18
  407.8 33.6 %reduce-scatter.2.cloned.1.call-done = bf16[128,448]{0,1:T(8,128)(2,1)} async-done(((bf16[128,3584]{0,1:T(8,128)(2,1)}), bf16[128,448]{0,1:T(8,128)(2,1)}) %reduce-scatter.2.cloned.1.call-update) | async-done | bytes 114704 | tf_op jit(solution)/shard_map/reduce_scatter | solution.py:56
  (2 shorter events, 0.0 us)
Async XLA Ops:
  7.2 389.6 %copy-start = (bf16[128,3584]{1,0:T(8,128)(2,1)S(1)}, bf16[128,3584]{1,0:T(8,128)(2,1)}, u32[]{:S(2)}) copy-start(bf16[128,3584]{1,0:T(8,128)(2,1)} %param.6) | copy-start | bytes 2752516
  7.2 315.1 %all-gather.2.cloned.1.call-start = ((), (), s32[]{:S(2)}) async-start(), calls=%async_computation.1 | async-start | bytes 9535488 | tf_op jit(solution)/shard_map/all_gather | solution.py:24
  7.9 433.5 %reduce-scatter.2.cloned.1.call-start = ((), (), s32[]{:S(2)}) async-start(), calls=%async_computation.2 | async-start | bytes 1032192 | tf_op jit(solution)/shard_map/reduce_scatter | solution.py:56
Sparse Core Ops, SparseCore 0:
  11.7 132.4 all-gather.1
  407.0 34.4 reduce-scatter.1
where the time goes:
time: 453 us; the launch traced here: 448 us
  blocking collectives  308 us (68%)
  local copies, waits for them, and re-layouts  71.8 us (16%)
  waiting for transfers between devices  34.3 us (8%)
  between operations  14.8 us (3%)
  matrix products  10.1 us (2%)
  other arithmetic  9.61 us (2%)
    unnamed x1, blocking collectives  185 us
    all_gather x1, blocking collectives, per_device(): lax.all_gather(blk_rows, 'fsdp', axis=0, tiled=True)  67.6 us
    all_gather x1, blocking collectives, per_device(): lax.all_gather(blk_cols, 'fsdp', axis=0, tiled=True)  55.1 us
    scatter x1, local copies, waits for them, and re-layouts, per_device(): dense_tile = jnp.zeros((row_blocks, col_blocks, block, block), jnp.bfloat...  46.1 us
    reduce_scatter x1, waiting for transfers between devices, per_device(): lax.psum_scatter(partial_value.astype(jnp.bfloat16), 'tp', scatter_dimens...  33.6 us
    transpose x1, local copies, waits for them, and re-layouts, per_device(): dense_tile.transpose(0, 2, 1, 3).reshape(model_width, col_blocks * block)  12.6 us
  transfers between devices with their start and end apart: 2, of which 1 were waited for; matrix products, arithmetic and copies ran while one was open for 2% of the time, Pallas kernels for 0%

commit v1 on v0

v1 whole, which is shorter than its diff:
```python
import math

import jax
import jax.numpy as jnp
from jax import lax
from jax.experimental import pallas as pl
from jax.experimental.pallas import tpu as pltpu
from jax.sharding import PartitionSpec as P

gelu_scale = math.sqrt(2.0 / math.pi)

BLK = 128
CAP = 3
META = 16
UNIT = CAP * BLK + META
NX = 4
NZ = 12
NC = 2
PLACES = [(z, x, c) for z in range(NZ) for x in range(NX) for c in range(NC)]


def place(z, x, c):
    return ((z % NZ) * NX + x % NX) * NC + c % NC


def shift(value, move):
    pairs = [(place(*p), place(*move(*p))) for p in PLACES]
    return lax.ppermute(value, "fsdp", pairs)


def up(value):
    return shift(value, lambda z, x, c: (z + 1, x, c))


def down(value):
    return shift(value, lambda z, x, c: (z - 1, x, c))


def apart(value):
    return shift(value, lambda z, x, c: (z + 1 - 2 * c, x, c))


def sibling(value):
    return shift(value, lambda z, x, c: (z, x, 1 - c))


def gelu_parts(preact):
    cube = preact * preact * preact
    tangent = jnp.tanh(gelu_scale * (preact + 0.044715 * cube))
    activated = 0.5 * preact * (1.0 + tangent)
    derivative = 0.5 * (1.0 + tangent) + 0.5 * preact * (1.0 - tangent * tangent) * gelu_scale * (
        1.0 + 3.0 * 0.044715 * preact * preact
    )
    return (activated, derivative)


def pack(w_blocks, blk_rows, blk_cols, counts):
    live = jnp.arange(CAP, dtype=jnp.int32) < counts.reshape(1)
    blocks = jnp.where(live[:, None, None], w_blocks.reshape(CAP, BLK, BLK), jnp.bfloat16(0))
    places = jnp.concatenate([blk_rows.reshape(CAP), blk_cols.reshape(CAP)]).astype(jnp.bfloat16)
    meta = jnp.pad(places[None, :], ((0, META - 1), (0, BLK - 2 * CAP)))
    return jnp.concatenate([blocks.reshape(CAP * BLK, BLK), meta], axis=0)


def places_of(units):
    n = units.shape[0] // UNIT
    return units.reshape(n, UNIT, BLK)[:, CAP * BLK, : 2 * CAP].astype(jnp.int32)


def scatter_kernel(sizes, *refs):
    n = len(sizes)
    places, sources = refs[0], refs[1 : 1 + n]
    dense, sems = refs[2 + n], refs[3 + n]
    base = 0
    for i, size in enumerate(sizes):
        source = sources[i]

        def one(u, _, source=source, base=base, i=i):
            for s in range(CAP):
                at = (base + u) * (2 * CAP) + s
                row = pl.multiple_of(places[at] * BLK, BLK)
                col = pl.multiple_of(places[at + CAP] * BLK, BLK)
                start = pl.multiple_of(u * UNIT + s * BLK, 16)
                pltpu.make_async_copy(
                    source.at[pl.ds(start, BLK), :],
                    dense.at[pl.ds(row, BLK), pl.ds(col, BLK)],
                    sems.at[i],
                ).start()
            return 0

        lax.fori_loop(0, size, one, 0)
        base += size
    for i, size in enumerate(sizes):
        whole = sources[i].at[pl.ds(0, size * CAP * BLK), :]
        pltpu.make_async_copy(whole, whole, sems.at[i]).wait()


def scatter(dense, stacks):
    sizes = [s.shape[0] // UNIT for s in stacks]
    places = jnp.concatenate([places_of(s) for s in stacks], axis=0).reshape(-1)
    n = len(stacks)
    moved = sum(sizes) * CAP * BLK * BLK * 2
    return pl.pallas_call(
        lambda *refs: scatter_kernel(sizes, *refs),
        out_shape=jax.ShapeDtypeStruct(dense.shape, dense.dtype),
        in_specs=[pl.BlockSpec(memory_space=pltpu.SMEM)]
        + [pl.BlockSpec(memory_space=pl.ANY)] * (n + 1),
        out_specs=pl.BlockSpec(memory_space=pl.ANY),
        scratch_shapes=[pltpu.SemaphoreType.DMA((n,))],
        input_output_aliases={n + 1: 0},
        cost_estimate=pl.CostEstimate(flops=0, bytes_accessed=4 * moved, transcendentals=0),
    )(places, *stacks, dense)


def per_device(tokens, cotangent, w_blocks, blk_rows, blk_cols, counts):
    tokens_here, model_width = tokens.shape
    shard = cotangent.shape[1]
    mine = pack(w_blocks, blk_rows, blk_cols, counts)
    by_x = [[place(z, x, c) for x in range(NX)] for z in range(NZ) for c in range(NC)]
    row = lax.all_gather(mine, "fsdp", axis=0, tiled=True, axis_index_groups=by_x)
    dense = jnp.zeros((model_width, shard), jnp.bfloat16)

    above, below = row, row
    held = [row]
    for step in range(5):
        above, below = up(above), down(below)
        held += [above, below]
    far = apart(lax.select(jnp.full(above.shape, lax.axis_index("fsdp") % NC == 0), above, below))
    first, second = held[:7], held[7:] + [far]
    dense = scatter(dense, first + [sibling(jnp.concatenate(first, axis=0))])
    dense = scatter(dense, second + [sibling(jnp.concatenate(second, axis=0))])

    preact = jnp.dot(tokens, dense, preferred_element_type=jnp.float32)
    activated, derivative = gelu_parts(preact)
    dpre = (cotangent.astype(jnp.float32) * derivative).astype(jnp.bfloat16)
    partial_value = lax.dot_general(
        dpre, dense, (((1,), (1,)), ((), ())), preferred_element_type=jnp.float32
    ).astype(jnp.bfloat16)
    n_tp = lax.axis_size("tp")
    pieces = partial_value.reshape(tokens_here, n_tp, model_width // n_tp).transpose(1, 0, 2)
    terms = lax.all_to_all(pieces, "tp", split_axis=0, concat_axis=0, tiled=True)
    summed = jnp.sum(terms.astype(jnp.float32), axis=0).astype(jnp.bfloat16)
    return (activated.astype(jnp.bfloat16), summed)


def solution(mesh):
    return jax.shard_map(
        per_device,
        mesh=mesh,
        in_specs=(
            P("fsdp", None),
            P("fsdp", "tp"),
            P("fsdp", "tp", None, None, None),
            P("fsdp", "tp", None),
            P("fsdp", "tp", None),
            P("fsdp", "tp"),
        ),
        out_specs=(P("fsdp", "tp"), P("fsdp", "tp")),
        check_vma=False,
    )
```

time: 453 us -> 463 us (1.022)
  blocking collectives: 308 us -> 10.8 us
  Pallas kernels: 0 us -> 290 us
  starting transfers between devices: 0.08 us -> 67.9 us
  local copies, waits for them, and re-layouts: 71.8 us -> 27.8 us
  between operations: 14.8 us -> 1.74 us
  waiting for transfers between devices: 34.3 us -> 45.2 us
  other arithmetic: 9.61 us -> 3.48 us
  matrix products: 10.1 us -> 15.8 us
    pallas_call x0 -> x2, Pallas kernels: none -> 290 us  [scatter(): pl.pallas_call(lambda *refs: scatter_kernel(sizes, *refs), out_shape=jax....]
    unnamed x1 -> x0, blocking collectives: 185 us -> none
    all_gather x2 -> x1, blocking collectives: 123 us -> 10.8 us  [per_device(): lax.all_gather(mine, 'fsdp', axis=0, tiled=True, axis_index_groups=by_x)]
    ppermute x0 -> x13, starting transfers between devices: none -> 61 us  [shift(): return lax.ppermute(value, 'fsdp', pairs)]
    scatter x1 -> x0, local copies, waits for them, and re-layouts: 46.1 us -> none  [per_device(): dense_tile = jnp.zeros((row_blocks, col_blocks, block, block), jnp.bfloat...]
    reduce_scatter x1 -> x0, waiting for transfers between devices: 33.6 us -> none  [per_device(): lax.psum_scatter(partial_value.astype(jnp.bfloat16), 'tp', scatter_dimens...]
    all_to_all x0 -> x1, waiting for transfers between devices: none -> 25.4 us  [per_device(): lax.all_to_all(pieces, 'tp', split_axis=0, concat_axis=0, tiled=True)]
    ppermute x0 -> x13, waiting for transfers between devices: none -> 19.8 us  [shift(): return lax.ppermute(value, 'fsdp', pairs)]
  transfers between devices with their start and end apart: 2 -> 14, of which waited for: 1 -> 6; matrix products, arithmetic and copies ran while one was open for 2% -> 6% of each run, Pallas kernels for 0% -> 36%
where the time goes in v1:
time: 463 us; the launch traced here: 462 us
  Pallas kernels  290 us (63%)
  starting transfers between devices  67.9 us (15%)
  waiting for transfers between devices  45.2 us (10%)
  local copies, waits for them, and re-layouts  27.8 us (6%)
  matrix products  15.8 us (3%)
  blocking collectives  10.8 us (2%)
    pallas_call x2, Pallas kernels, scatter(): pl.pallas_call(lambda *refs: scatter_kernel(sizes, *refs), out_shape=jax....  290 us
    ppermute x13, starting transfers between devices, shift(): return lax.ppermute(value, 'fsdp', pairs)  61 us
    all_to_all x1, waiting for transfers between devices, per_device(): lax.all_to_all(pieces, 'tp', split_axis=0, concat_axis=0, tiled=True)  25.4 us
    ppermute x13, waiting for transfers between devices, shift(): return lax.ppermute(value, 'fsdp', pairs)  19.8 us
    all_gather x1, blocking collectives, per_device(): lax.all_gather(mine, 'fsdp', axis=0, tiled=True, axis_index_groups=by_x)  10.8 us
    unnamed x53, local copies, waits for them, and re-layouts  10.4 us
  transfers between devices with their start and end apart: 14, of which 6 were waited for; matrix products, arithmetic and copies ran while one was open for 6% of the time, Pallas kernels for 36%

profile of v1, /device:TPU:1, one launch (start us, length us, event | category | flops | bytes accessed | tf_op | source)
XLA Modules:
  0.0 462.3 jit_solution(15616589387317866015)
XLA Ops:
  2.2 1.0 bitcast_select_fusion
  3.2 10.8 %all_gather.3.refs_1_ = bf16[1600,128]{1,0:T(8,128)(2,1)S(1)} all-gather(bf16[400,128]{1,0:T(8,128)(2,1)S(1)} %pad_maximum_fusion), channel_id=1, replica_groups={{0,16,32,48},{8,24,40,56},{64,80,96,112},{72,88,104,120},{128,144,160,1..., dimensions={0}, use_global_device_ids=true | all-gather | bytes 512000 | tf_op jit(solution)/shard_map/all_gather | solution.py:120
  14.1 5.1 %collective-permute-start = (bf16[1600,128]{1,0:T(8,128)(2,1)S(1)}, bf16[1600,128]{1,0:T(8,128)(2,1)S(1)}, u32[]{:S(2)}, u32[]{:S(2)}) collective-permute-start(bf16[1600,128]{1,0:T(8,128)(2,1)S(1)} %all_gather.3.refs_1_), channel_id=1, source_target_pairs={{0,64},{8,72},{16,80},{24,88},{32,96},{40,104},{48,112},{56,120},{... | collective-permute-start | bytes 1228808 | tf_op jit(solution)/shard_map/ppermute | solution.py:28
  19.2 12.2 %collective-permute-start.4 = (bf16[1600,128]{1,0:T(8,128)(2,1)S(1)}, bf16[1600,128]{1,0:T(8,128)(2,1)S(1)}, u32[]{:S(2)}, u32[]{:S(2)}) collective-permute-start(bf16[1600,128]{1,0:T(8,128)(2,1)S(1)} %all_gather.3.refs_1_), channel_id=1, source_target_pairs={{0,704},{8,712},{16,720},{24,728},{32,736},{40,744},{48,752},{56,7... | collective-permute-start | bytes 1228808 | tf_op jit(solution)/shard_map/ppermute | solution.py:28
  32.3 4.6 collective-permute-done.refs_2_
  36.8 1.9 collective-permute-start.1
  38.8 4.6 collective-permute-start.5
  44.9 2.9 collective-permute-done.1.refs_4_
  47.8 1.9 collective-permute-start.2
  49.8 4.6 collective-permute-start.6
  55.9 1.8 collective-permute-done.2.refs_6_
  57.7 1.9 collective-permute-start.3
  59.7 4.6 collective-permute-start.7
  65.8 7.6 %collective-permute-start.12 = (bf16[11200,128]{1,0:T(8,128)(2,1)}, bf16[11200,128]{1,0:T(8,128)(2,1)}, u32[]{:S(2)}, u32[]{:S(2)}) collective-permute-start(bf16[11200,128]{1,0:T(8,128)(2,1)} %constant_dynamic-update-slice_fusion.5), channel_id=1, source_target_pairs={{0,8},{8,0},{16,24},{24,16},{32,40},{40,32},{48,56},{56,48},{64,72... | collective-permute-start | bytes 8601608 | tf_op jit(solution)/shard_map/ppermute | solution.py:28
  73.5 1.9 collective-permute-start.8
  75.4 4.6 collective-permute-start.9
  81.5 5.6 %collective-permute-done.8.refs_3_ = bf16[1600,128]{1,0:T(8,128)(2,1)S(1)} collective-permute-done((bf16[1600,128]{1,0:T(8,128)(2,1)S(1)}, bf16[1600,128]{1,0:T(8,128)(2,1)S(1)}, u32[]{:S(2)}, u32[]{:S(2)}) %collective-permute-start.8) | collective-permute-done | bytes 409632 | tf_op jit(solution)/shard_map/ppermute | solution.py:28
  88.0 0.9 constant_dynamic-update-slice_fusion.1
  88.9 5.3 %collective-permute-start.10 = (bf16[1600,128]{1,0:T(8,128)(2,1)S(1)}, bf16[1600,128]{1,0:T(8,128)(2,1)S(1)}, u32[]{:S(2)}, u32[]{:S(2)}) collective-permute-start(bf16[1600,128]{1,0:T(8,128)(2,1)S(1)} %get-tuple-element.7), channel_id=1, source_target_pairs={{0,64},{8,712},{16,80},{24,728},{32,96},{40,744},{48,112},{56,760}... | collective-permute-start | bytes 1228808 | tf_op jit(solution)/shard_map/ppermute | solution.py:28
  94.3 4.9 %collective-permute-done.10.refs_5_ = bf16[1600,128]{1,0:T(8,128)(2,1)S(1)} collective-permute-done((bf16[1600,128]{1,0:T(8,128)(2,1)S(1)}, bf16[1600,128]{1,0:T(8,128)(2,1)S(1)}, u32[]{:S(2)}, u32[]{:S(2)}) %collective-permute-start.10) | collective-permute-done | bytes 409632 | tf_op jit(solution)/shard_map/ppermute | solution.py:28
  99.1 0.8 constant_dynamic-update-slice_fusion
  100.0 4.8 %collective-permute-start.11 = (bf16[8000,128]{1,0:T(8,128)(2,1)}, bf16[8000,128]{1,0:T(8,128)(2,1)}, u32[]{:S(2)}, u32[]{:S(2)}) collective-permute-start(bf16[8000,128]{1,0:T(8,128)(2,1)} %constant_dynamic-update-slice_fusion), channel_id=1, source_target_pairs={{0,8},{8,0},{16,24},{24,16},{32,40},{40,32},{48,56},{56,48},{64,72... | collective-permute-start | bytes 6144008 | tf_op jit(solution)/shard_map/ppermute | solution.py:28
  105.0 2.0 copy.58
  114.4 5.4 %broadcast_in_dim.29.refs_9_ = bf16[3584,1792]{1,0:T(8,128)(2,1)} broadcast(bf16[]{:T(256)} %constant.11.clone.1), dimensions={} | broadcast | bytes 12845058 | tf_op jit(solution)/shard_map/broadcast_in_dim | solution.py:121
  119.8 168.6 %shard_map.77.refs_7_ = bf16[3584,1792]{1,0:T(8,128)(2,1)} custom-call(s32[336]{0:T(512)} %reshape.157.refs_0_, bf16[1600,128]{1,0:T(8,128)(2,1)} %copy-done.2, bf16[1600,128]{1,0:T(8,128)(2,1)} %copy-done.3, bf16[1600,128]{1,0:T(8,128)(2,1)} %copy-done.4, bf16[1600,128]{1,0:T(8,128)(2,1)} %copy-done.5, ...), custom_call_target="tpu_custom_call", output_to_operand_aliasing={{}: (9, {})} | custom-call | bytes 22020096 | tf_op jit(solution)/shard_map/pallas_call | solution.py:103
  290.2 121.0 %shard_map.78 = bf16[3584,1792]{1,0:T(8,128)(2,1)} custom-call(s32[240]{0:T(256)} %reshape.155.refs_0_, bf16[1600,128]{1,0:T(8,128)(2,1)} %copy-done.7, bf16[1600,128]{1,0:T(8,128)(2,1)} %copy-done.8, bf16[1600,128]{1,0:T(8,128)(2,1)} %copy-done.1, bf16[1600,128]{1,0:T(8,128)(2,1)} %copy-done.11, ...), custom_call_target="tpu_custom_call", output_to_operand_aliasing={{}: (7, {})} | custom-call | bytes 15728640 | tf_op jit(solution)/shard_map/pallas_call | solution.py:103
  411.2 6.7 %multiply_convert_fusion = (bf16[128,1792]{0,1:T(8,128)(2,1)S(1)}, f32[128,1792]{0,1:T(8,128)S(1)}) fusion(bf16[3584,1792]{1,0:T(8,128)(2,1)} %shard_map.78, bf16[128,3584]{1,0:T(8,128)(2,1)S(1)} %copy-done), kind=kOutput, calls=%fused_computation.13 | convolution fusion | flops 1646231552 | bytes 15138816 | tf_op jit(solution)/shard_map/dot_general | solution.py:133
  417.9 9.1 %convolution_convert_fusion = bf16[128,3584]{1,0:T(8,128)(2,1)S(1)} fusion(bf16[3584,1792]{1,0:T(8,128)(2,1)} %shard_map.78, f32[128,1792]{0,1:T(8,128)S(1)} %get-tuple-element.9, bf16[128,1792]{0,1:T(8,128)(2,1)S(1)} %copy-done.13), kind=kOutput, calls=%fused_computation | convolution fusion | flops 1649213440 | bytes 15138816 | tf_op jit(solution)/shard_map/dot_general | solution.py:136
  427.0 1.3 copy.59
  428.3 6.8 %all-to-all-start = ((bf16[8,128,448]{1,2,0:T(8,128)(2,1)}), bf16[8,128,448]{1,2,0:T(8,128)(2,1)S(1)}, u32[]{:S(2)}, u32[]{:S(2)}) async-start(bf16[8,128,448]{1,2,0:T(8,128)(2,1)} %bitcast.35), calls=%async_computation | async-start | bytes 1835008 | tf_op jit(solution)/shard_map/all_to_all | solution.py:141
  435.1 1.0 copy.60
  436.1 25.4 %all-to-all-done = bf16[8,128,448]{1,2,0:T(8,128)(2,1)S(1)} async-done(((bf16[8,128,448]{1,2,0:T(8,128)(2,1)}), bf16[8,128,448]{1,2,0:T(8,128)(2,1)S(1)}, u32[]{:S(2)}, u32[]{:S(2)}) %all-to-all-start) | async-done | bytes 917536 | tf_op jit(solution)/shard_map/all_to_all | solution.py:141
  (100 shorter events, 18.9 us)
Async XLA Ops:
  0.6 410.6 %copy-start = (bf16[128,3584]{1,0:T(8,128)(2,1)S(1)}, bf16[128,3584]{1,0:T(8,128)(2,1)}, u32[]{:S(2)}) copy-start(bf16[128,3584]{1,0:T(8,128)(2,1)} %param.6) | copy-start | bytes 2752516
  14.1 90.7 %copy-start.2 = (bf16[1600,128]{1,0:T(8,128)(2,1)}, bf16[1600,128]{1,0:T(8,128)(2,1)S(1)}, u32[]{:S(2)}) copy-start(bf16[1600,128]{1,0:T(8,128)(2,1)S(1)} %all_gather.3.refs_1_) | copy-start | bytes 1228804
  14.1 22.8 %collective-permute-start = (bf16[1600,128]{1,0:T(8,128)(2,1)S(1)}, bf16[1600,128]{1,0:T(8,128)(2,1)S(1)}, u32[]{:S(2)}, u32[]{:S(2)}) collective-permute-start(bf16[1600,128]{1,0:T(8,128)(2,1)S(1)} %all_gather.3.refs_1_), channel_id=1, source_target_pairs={{0,64},{8,72},{16,80},{24,88},{32,96},{40,104},{48,112},{56,120},{... | collective-permute-start | bytes 1228808 | tf_op jit(solution)/shard_map/ppermute | solution.py:28
  19.2 19.5 %collective-permute-start.4 = (bf16[1600,128]{1,0:T(8,128)(2,1)S(1)}, bf16[1600,128]{1,0:T(8,128)(2,1)S(1)}, u32[]{:S(2)}, u32[]{:S(2)}) collective-permute-start(bf16[1600,128]{1,0:T(8,128)(2,1)S(1)} %all_gather.3.refs_1_), channel_id=1, source_target_pairs={{0,704},{8,712},{16,720},{24,728},{32,736},{40,744},{48,752},{56,7... | collective-permute-start | bytes 1228808 | tf_op jit(solution)/shard_map/ppermute | solution.py:28
  36.8 70.1 %copy-start.3 = (bf16[1600,128]{1,0:T(8,128)(2,1)}, bf16[1600,128]{1,0:T(8,128)(2,1)S(1)}, u32[]{:S(2)}) copy-start(bf16[1600,128]{1,0:T(8,128)(2,1)S(1)} %collective-permute-done.refs_2_) | copy-start | bytes 1228804
  36.8 11.0 %collective-permute-start.1 = (bf16[1600,128]{1,0:T(8,128)(2,1)S(1)}, bf16[1600,128]{1,0:T(8,128)(2,1)S(1)}, u32[]{:S(2)}, u32[]{:S(2)}) collective-permute-start(bf16[1600,128]{1,0:T(8,128)(2,1)S(1)} %collective-permute-done.refs_2_), channel_id=1, source_target_pairs={{0,64},{8,72},{16,80},{24,88},{32,96},{40,104},{48,112},{56,120},{... | collective-permute-start | bytes 1228808 | tf_op jit(solution)/shard_map/ppermute | solution.py:28
  38.8 68.3 %copy-start.4 = (bf16[1600,128]{1,0:T(8,128)(2,1)}, bf16[1600,128]{1,0:T(8,128)(2,1)S(1)}, u32[]{:S(2)}) copy-start(bf16[1600,128]{1,0:T(8,128)(2,1)S(1)} %collective-permute-done.4.refs_3_) | copy-start | bytes 1228804
  38.8 11.0 %collective-permute-start.5 = (bf16[1600,128]{1,0:T(8,128)(2,1)S(1)}, bf16[1600,128]{1,0:T(8,128)(2,1)S(1)}, u32[]{:S(2)}, u32[]{:S(2)}) collective-permute-start(bf16[1600,128]{1,0:T(8,128)(2,1)S(1)} %collective-permute-done.4.refs_3_), channel_id=1, source_target_pairs={{0,704},{8,712},{16,720},{24,728},{32,736},{40,744},{48,752},{56,7... | collective-permute-start | bytes 1228808 | tf_op jit(solution)/shard_map/ppermute | solution.py:28
  47.8 59.4 %copy-start.5 = (bf16[1600,128]{1,0:T(8,128)(2,1)}, bf16[1600,128]{1,0:T(8,128)(2,1)S(1)}, u32[]{:S(2)}) copy-start(bf16[1600,128]{1,0:T(8,128)(2,1)S(1)} %collective-permute-done.1.refs_4_) | copy-start | bytes 1228804
  47.8 9.9 %collective-permute-start.2 = (bf16[1600,128]{1,0:T(8,128)(2,1)S(1)}, bf16[1600,128]{1,0:T(8,128)(2,1)S(1)}, u32[]{:S(2)}, u32[]{:S(2)}) collective-permute-start(bf16[1600,128]{1,0:T(8,128)(2,1)S(1)} %collective-permute-done.1.refs_4_), channel_id=1, source_target_pairs={{0,64},{8,72},{16,80},{24,88},{32,96},{40,104},{48,112},{56,120},{... | collective-permute-start | bytes 1228808 | tf_op jit(solution)/shard_map/ppermute | solution.py:28
  49.7 57.6 %copy-start.6 = (bf16[1600,128]{1,0:T(8,128)(2,1)}, bf16[1600,128]{1,0:T(8,128)(2,1)S(1)}, u32[]{:S(2)}) copy-start(bf16[1600,128]{1,0:T(8,128)(2,1)S(1)} %collective-permute-done.5.refs_5_) | copy-start | bytes 1228804
  49.8 9.9 %collective-permute-start.6 = (bf16[1600,128]{1,0:T(8,128)(2,1)S(1)}, bf16[1600,128]{1,0:T(8,128)(2,1)S(1)}, u32[]{:S(2)}, u32[]{:S(2)}) collective-permute-start(bf16[1600,128]{1,0:T(8,128)(2,1)S(1)} %collective-permute-done.5.refs_5_), channel_id=1, source_target_pairs={{0,704},{8,712},{16,720},{24,728},{32,736},{40,744},{48,752},{56,7... | collective-permute-start | bytes 1228808 | tf_op jit(solution)/shard_map/ppermute | solution.py:28
  57.7 30.3 %copy-start.9 = (bf16[1600,128]{1,0:T(8,128)(2,1)}, bf16[1600,128]{1,0:T(8,128)(2,1)S(1)}, u32[]{:S(2)}) copy-start(bf16[1600,128]{1,0:T(8,128)(2,1)S(1)} %collective-permute-done.2.refs_6_) | copy-start | bytes 1228804
  57.7 15.7 %collective-permute-start.3 = (bf16[1600,128]{1,0:T(8,128)(2,1)S(1)}, bf16[1600,128]{1,0:T(8,128)(2,1)S(1)}, u32[]{:S(2)}, u32[]{:S(2)}) collective-permute-start(bf16[1600,128]{1,0:T(8,128)(2,1)S(1)} %collective-permute-done.2.refs_6_), channel_id=1, source_target_pairs={{0,64},{8,72},{16,80},{24,88},{32,96},{40,104},{48,112},{56,120},{... | collective-permute-start | bytes 1228808 | tf_op jit(solution)/shard_map/ppermute | solution.py:28
  59.6 28.3 %copy-start.10 = (bf16[1600,128]{1,0:T(8,128)(2,1)}, bf16[1600,128]{1,0:T(8,128)(2,1)S(1)}, u32[]{:S(2)}) copy-start(bf16[1600,128]{1,0:T(8,128)(2,1)S(1)} %collective-permute-done.6.refs_7_) | copy-start | bytes 1228804
  59.7 15.7 %collective-permute-start.7 = (bf16[1600,128]{1,0:T(8,128)(2,1)S(1)}, bf16[1600,128]{1,0:T(8,128)(2,1)S(1)}, u32[]{:S(2)}, u32[]{:S(2)}) collective-permute-start(bf16[1600,128]{1,0:T(8,128)(2,1)S(1)} %collective-permute-done.6.refs_7_), channel_id=1, source_target_pairs={{0,704},{8,712},{16,720},{24,728},{32,736},{40,744},{48,752},{56,7... | collective-permute-start | bytes 1228808 | tf_op jit(solution)/shard_map/ppermute | solution.py:28
  65.8 46.7 %collective-permute-start.12 = (bf16[11200,128]{1,0:T(8,128)(2,1)}, bf16[11200,128]{1,0:T(8,128)(2,1)}, u32[]{:S(2)}, u32[]{:S(2)}) collective-permute-start(bf16[11200,128]{1,0:T(8,128)(2,1)} %constant_dynamic-update-slice_fusion.5), channel_id=1, source_target_pairs={{0,8},{8,0},{16,24},{24,16},{32,40},{40,32},{48,56},{56,48},{64,72... | collective-permute-start | bytes 8601608 | tf_op jit(solution)/shard_map/ppermute | solution.py:28
  73.4 13.7 %copy-start.7 = (bf16[1600,128]{1,0:T(8,128)(2,1)}, bf16[1600,128]{1,0:T(8,128)(2,1)S(1)}, u32[]{:S(2)}) copy-start(bf16[1600,128]{1,0:T(8,128)(2,1)S(1)} %collective-permute-done.3.refs_1_) | copy-start | bytes 1228804
  73.5 13.7 %collective-permute-start.8 = (bf16[1600,128]{1,0:T(8,128)(2,1)S(1)}, bf16[1600,128]{1,0:T(8,128)(2,1)S(1)}, u32[]{:S(2)}, u32[]{:S(2)}) collective-permute-start(bf16[1600,128]{1,0:T(8,128)(2,1)S(1)} %collective-permute-done.3.refs_1_), channel_id=1, source_target_pairs={{0,64},{8,72},{16,80},{24,88},{32,96},{40,104},{48,112},{56,120},{... | collective-permute-start | bytes 1228808 | tf_op jit(solution)/shard_map/ppermute | solution.py:28
  75.4 12.6 %copy-start.8 = (bf16[1600,128]{1,0:T(8,128)(2,1)}, bf16[1600,128]{1,0:T(8,128)(2,1)S(1)}, u32[]{:S(2)}) copy-start(bf16[1600,128]{1,0:T(8,128)(2,1)S(1)} %collective-permute-done.7.refs_2_) | copy-start | bytes 1228804
  75.4 12.6 %collective-permute-start.9 = (bf16[1600,128]{1,0:T(8,128)(2,1)S(1)}, bf16[1600,128]{1,0:T(8,128)(2,1)S(1)}, u32[]{:S(2)}, u32[]{:S(2)}) collective-permute-start(bf16[1600,128]{1,0:T(8,128)(2,1)S(1)} %collective-permute-done.7.refs_2_), channel_id=1, source_target_pairs={{0,704},{8,712},{16,720},{24,728},{32,736},{40,744},{48,752},{56,7... | collective-permute-start | bytes 1228808 | tf_op jit(solution)/shard_map/ppermute | solution.py:28
  87.1 32.6 %copy-start.1 = (bf16[1600,128]{1,0:T(8,128)(2,1)}, bf16[1600,128]{1,0:T(8,128)(2,1)S(1)}, u32[]{:S(2)}) copy-start(bf16[1600,128]{1,0:T(8,128)(2,1)S(1)} %collective-permute-done.8.refs_3_) | copy-start | bytes 1228804
  88.0 16.8 %copy-start.11 = (bf16[1600,128]{1,0:T(8,128)(2,1)}, bf16[1600,128]{1,0:T(8,128)(2,1)S(1)}, u32[]{:S(2)}) copy-start(bf16[1600,128]{1,0:T(8,128)(2,1)S(1)} %collective-permute-done.9.refs_4_) | copy-start | bytes 1228804
  88.9 10.2 %collective-permute-start.10 = (bf16[1600,128]{1,0:T(8,128)(2,1)S(1)}, bf16[1600,128]{1,0:T(8,128)(2,1)S(1)}, u32[]{:S(2)}, u32[]{:S(2)}) collective-permute-start(bf16[1600,128]{1,0:T(8,128)(2,1)S(1)} %get-tuple-element.7), channel_id=1, source_target_pairs={{0,64},{8,712},{16,80},{24,728},{32,96},{40,744},{48,112},{56,760}... | collective-permute-start | bytes 1228808 | tf_op jit(solution)/shard_map/ppermute | solution.py:28
  99.1 5.7 %copy-start.12 = (bf16[1600,128]{1,0:T(8,128)(2,1)}, bf16[1600,128]{1,0:T(8,128)(2,1)S(1)}, u32[]{:S(2)}) copy-start(bf16[1600,128]{1,0:T(8,128)(2,1)S(1)} %collective-permute-done.10.refs_5_) | copy-start | bytes 1228804
  100.0 188.5 %collective-permute-start.11 = (bf16[8000,128]{1,0:T(8,128)(2,1)}, bf16[8000,128]{1,0:T(8,128)(2,1)}, u32[]{:S(2)}, u32[]{:S(2)}) collective-permute-start(bf16[8000,128]{1,0:T(8,128)(2,1)} %constant_dynamic-update-slice_fusion), channel_id=1, source_target_pairs={{0,8},{8,0},{16,24},{24,16},{32,40},{40,32},{48,56},{56,48},{64,72... | collective-permute-start | bytes 6144008 | tf_op jit(solution)/shard_map/ppermute | solution.py:28
  411.2 6.7 %copy-start.13 = (bf16[128,1792]{0,1:T(8,128)(2,1)S(1)}, bf16[128,1792]{0,1:T(8,128)(2,1)}, u32[]{:S(2)}) copy-start(bf16[128,1792]{0,1:T(8,128)(2,1)} %copy.58) | copy-start | bytes 1376260
  428.3 33.2 %all-to-all-start = ((bf16[8,128,448]{1,2,0:T(8,128)(2,1)}), bf16[8,128,448]{1,2,0:T(8,128)(2,1)S(1)}, u32[]{:S(2)}, u32[]{:S(2)}) async-start(bf16[8,128,448]{1,2,0:T(8,128)(2,1)} %bitcast.35), calls=%async_computation | async-start | bytes 1835008 | tf_op jit(solution)/shard_map/all_to_all | solution.py:141

commit v2 on v1

v2 whole, which is shorter than its diff:
```python
import math

import jax
import jax.numpy as jnp
from jax import lax
from jax.experimental import pallas as pl
from jax.experimental.pallas import tpu as pltpu
from jax.sharding import PartitionSpec as P

gelu_scale = math.sqrt(2.0 / math.pi)

BLK = 128
CAP = 3
META = 16
UNIT = CAP * BLK + META
NX = 4
NZ = 12
NC = 2
PLACES = [(z, x, c) for z in range(NZ) for x in range(NX) for c in range(NC)]


def place(z, x, c):
    return ((z % NZ) * NX + x % NX) * NC + c % NC


def shift(value, move):
    pairs = [(place(*p), place(*move(*p))) for p in PLACES]
    return lax.ppermute(value, "fsdp", pairs)


def up(value):
    return shift(value, lambda z, x, c: (z + 1, x, c))


def down(value):
    return shift(value, lambda z, x, c: (z - 1, x, c))


def apart(value):
    return shift(value, lambda z, x, c: (z + 1 - 2 * c, x, c))


def sibling(value):
    return shift(value, lambda z, x, c: (z, x, 1 - c))


def gelu_parts(preact):
    cube = preact * preact * preact
    tangent = jnp.tanh(gelu_scale * (preact + 0.044715 * cube))
    activated = 0.5 * preact * (1.0 + tangent)
    derivative = 0.5 * (1.0 + tangent) + 0.5 * preact * (1.0 - tangent * tangent) * gelu_scale * (
        1.0 + 3.0 * 0.044715 * preact * preact
    )
    return (activated, derivative)


def pack(w_blocks, blk_rows, blk_cols, counts):
    live = jnp.arange(CAP, dtype=jnp.int32) < counts.reshape(1)
    blocks = jnp.where(live[:, None, None], w_blocks.reshape(CAP, BLK, BLK), jnp.bfloat16(0))
    places = jnp.concatenate([blk_rows.reshape(CAP), blk_cols.reshape(CAP)]).astype(jnp.bfloat16)
    meta = jnp.pad(places[None, :], ((0, META - 1), (0, BLK - 2 * CAP)))
    return jnp.concatenate([blocks.reshape(CAP * BLK, BLK), meta], axis=0)


def fused_kernel(sizes, *refs):
    n = len(sizes)
    sources = refs[:n]
    tokens, cotangent, hidden, pieces = refs[n : n + 4]
    stage, dense, meta, places, dpre, sems, meta_sem = refs[n + 4 :]
    units = sum(sizes)

    def landing(i):
        first = sum(sizes[:i]) * UNIT
        return pltpu.make_async_copy(
            sources[i], stage.at[pl.ds(first, sizes[i] * UNIT), :], sems.at[i]
        )

    for i in range(n):
        landing(i).start()

    chunks, depth, width = dense.shape

    def clear(i, _):
        at = pl.multiple_of(i * 128, 128)
        for j in range(chunks):
            dense[j, pl.ds(at, 128), :] = jnp.zeros((128, width), jnp.bfloat16)
        return 0

    lax.fori_loop(0, depth // 128, clear, 0)
    for i in range(n):
        landing(i).wait()

    def read(u, _):
        at = pl.multiple_of(u * UNIT + CAP * BLK, META)
        rows = stage[pl.ds(at, META), :].astype(jnp.float32).astype(jnp.int32)
        meta[pl.ds(u, 1), :] = rows[:1]
        return 0

    lax.fori_loop(0, units, read, 0, unroll=8)
    fetch = pltpu.make_async_copy(meta, places, meta_sem)
    fetch.start()
    fetch.wait()

    def put(u, _):
        for s in range(CAP):
            row = pl.multiple_of(places[u, s] * BLK, BLK)
            col = places[u, CAP + s]
            chunk = lax.shift_right_logical(col, 1)
            lane = pl.multiple_of(jnp.bitwise_and(col, 1) * BLK, BLK)
            at = pl.multiple_of(u * UNIT + s * BLK, META)
            dense[chunk, pl.ds(row, BLK), pl.ds(lane, BLK)] = stage[pl.ds(at, BLK), :]
        return 0

    lax.fori_loop(0, units, put, 0, unroll=2)

    for j in range(chunks):
        here = slice(j * width, (j + 1) * width)
        preact = jnp.dot(tokens[...], dense[j], preferred_element_type=jnp.float32)
        activated, derivative = gelu_parts(preact)
        hidden[:, here] = activated.astype(jnp.bfloat16)
        dpre[:, here] = (cotangent[:, here].astype(jnp.float32) * derivative).astype(jnp.bfloat16)
    slab = pieces.shape[2]
    for d in range(pieces.shape[0]):
        total = jnp.zeros(pieces.shape[1:], jnp.float32)
        for j in range(chunks):
            total += lax.dot_general(
                dpre[:, j * width : (j + 1) * width],
                dense[j, d * slab : (d + 1) * slab, :],
                (((1,), (1,)), ((), ())),
                preferred_element_type=jnp.float32,
            )
        pieces[d] = total.astype(jnp.bfloat16)


def fused(stacks, tokens, cotangent, n_tp):
    sizes = [s.shape[0] // UNIT for s in stacks]
    n, units = len(sizes), sum(sizes)
    rows, model_width = tokens.shape
    shard = cotangent.shape[1]
    width = 2 * BLK
    vmem = pl.BlockSpec(memory_space=pltpu.VMEM)
    return pl.pallas_call(
        lambda *refs: fused_kernel(sizes, *refs),
        out_shape=(
            jax.ShapeDtypeStruct((rows, shard), jnp.bfloat16),
            jax.ShapeDtypeStruct((n_tp, rows, model_width // n_tp), jnp.bfloat16),
        ),
        in_specs=[pl.BlockSpec(memory_space=pl.ANY)] * n + [vmem, vmem],
        out_specs=(vmem, vmem),
        scratch_shapes=[
            pltpu.VMEM((units * UNIT, BLK), jnp.bfloat16),
            pltpu.VMEM((shard // width, model_width, width), jnp.bfloat16),
            pltpu.VMEM((units, BLK), jnp.int32),
            pltpu.SMEM((units, BLK), jnp.int32),
            pltpu.VMEM((rows, shard), jnp.bfloat16),
            pltpu.SemaphoreType.DMA((n,)),
            pltpu.SemaphoreType.DMA,
        ],
        compiler_params=pltpu.CompilerParams(vmem_limit_bytes=40 * 1024 * 1024),
        cost_estimate=pl.CostEstimate(
            flops=4 * rows * model_width * shard,
            bytes_accessed=2 * units * UNIT * BLK,
            transcendentals=rows * shard,
        ),
    )(*stacks, tokens, cotangent)


def per_device(tokens, cotangent, w_blocks, blk_rows, blk_cols, counts):
    mine = pack(w_blocks, blk_rows, blk_cols, counts)
    by_x = [[place(z, x, c) for x in range(NX)] for z in range(NZ) for c in range(NC)]
    row = lax.all_gather(mine, "fsdp", axis=0, tiled=True, axis_index_groups=by_x)

    above, below = row, row
    held = [row]
    for step in range(5):
        above, below = up(above), down(below)
        held += [above, below]
    far = apart(lax.select(jnp.full(above.shape, lax.axis_index("fsdp") % NC == 0), above, below))
    batches = [held[:5], held[5:9], held[9:]]
    others = [sibling(jnp.concatenate(b, axis=0)) for b in batches] + [sibling(far)]
    hidden, pieces = fused(held + [far] + others, tokens, cotangent, lax.axis_size("tp"))
    terms = lax.all_to_all(pieces, "tp", split_axis=0, concat_axis=0, tiled=True)
    summed = jnp.sum(terms.astype(jnp.float32), axis=0).astype(jnp.bfloat16)
    return (hidden, summed)


def solution(mesh):
    return jax.shard_map(
        per_device,
        mesh=mesh,
        in_specs=(
            P("fsdp", None),
            P("fsdp", "tp"),
            P("fsdp", "tp", None, None, None),
            P("fsdp", "tp", None),
            P("fsdp", "tp", None),
            P("fsdp", "tp"),
        ),
        out_specs=(P("fsdp", "tp"), P("fsdp", "tp")),
        check_vma=False,
    )
```

time: 463 us -> 152 us (0.33)
  Pallas kernels: 290 us -> 15.1 us
  blocking collectives: 10.8 us -> 42.6 us
  local copies, waits for them, and re-layouts: 27.8 us -> 0.96 us
  waiting for transfers between devices: 45.2 us -> 19.2 us
  matrix products: 15.8 us -> 0 us
    pallas_call x2 -> x1, Pallas kernels: 290 us -> 15.1 us  [fused(): pl.pallas_call(lambda *refs: fused_kernel(sizes, *refs), out_shape=(jax.S...]
    all_to_all x0 -> x1, blocking collectives: none -> 31.7 us  [per_device(): lax.all_to_all(pieces, 'tp', split_axis=0, concat_axis=0, tiled=True)]
    all_to_all x1 -> x0, waiting for transfers between devices: 25.4 us -> none  [per_device(): lax.all_to_all(pieces, 'tp', split_axis=0, concat_axis=0, tiled=True)]
    dot_general x2 -> x0, matrix products: 15.8 us -> none  [the longest x1 9.12 us: per_device(): lax.dot_general(dpre, dense, (((1,), (1,)), ((), ())), preferred_element_...]
    unnamed x53 -> x8, local copies, waits for them, and re-layouts: 10.4 us -> 0.21 us
    ppermute x13 -> x15, starting transfers between devices: 61 us -> 69 us  [shift(): return lax.ppermute(value, 'fsdp', pairs)]
    all_to_all x1 -> x0, starting transfers between devices: 6.83 us -> none  [per_device(): lax.all_to_all(pieces, 'tp', split_axis=0, concat_axis=0, tiled=True)]
    slice x14 -> x0, local copies, waits for them, and re-layouts: 5.85 us -> none  [places_of(): return units.reshape(n, UNIT, BLK)[:, CAP * BLK, :2 * CAP].astype(jnp.int32)]
  transfers between devices with their start and end apart: 14 -> 15, of which waited for: 6 -> 7; matrix products, arithmetic and copies ran while one was open for 6% -> 0% of each run, Pallas kernels for 36% -> 0%
where the time goes in v2:
time: 152 us; the launch traced here: 151 us
  starting transfers between devices  69 us (45%)
  blocking collectives  42.6 us (28%)
  waiting for transfers between devices  19.2 us (13%)
  Pallas kernels  15.1 us (10%)
  other arithmetic  2.76 us (2%)
  between operations  1.59 us (1%)
    ppermute x15, starting transfers between devices, shift(): return lax.ppermute(value, 'fsdp', pairs)  69 us
    all_to_all x1, blocking collectives, per_device(): lax.all_to_all(pieces, 'tp', split_axis=0, concat_axis=0, tiled=True)  31.7 us
    ppermute x15, waiting for transfers between devices, shift(): return lax.ppermute(value, 'fsdp', pairs)  19.2 us
    pallas_call x1, Pallas kernels, fused(): pl.pallas_call(lambda *refs: fused_kernel(sizes, *refs), out_shape=(jax.S...  15.1 us
    all_gather x1, blocking collectives, per_device(): lax.all_gather(mine, 'fsdp', axis=0, tiled=True, axis_index_groups=by_x)  10.8 us
  transfers between devices with their start and end apart: 15, of which 7 were waited for; matrix products, arithmetic and copies ran while one was open for 0% of the time, Pallas kernels for 0%

profile of v2, /device:TPU:1, one launch (start us, length us, event | category | flops | bytes accessed | tf_op | source)
XLA Modules:
  0.0 151.2 jit_solution(10575726203921990443)
XLA Ops:
  1.3 0.1 broadcast_bitcast_fusion
  1.4 0.7 convert_bitcast_fusion
  2.0 0.1 fusion.5
  2.1 1.0 bitcast_select_fusion
  3.1 10.8 %all_gather.3.refs_0_ = bf16[1600,128]{1,0:T(8,128)(2,1)S(1)} all-gather(bf16[400,128]{1,0:T(8,128)(2,1)S(1)} %pad_maximum_fusion.2), channel_id=1, replica_groups={{0,16,32,48},{8,24,40,56},{64,80,96,112},{72,88,104,120},{128,144,160,1..., dimensions={0}, use_global_device_ids=true | all-gather | bytes 512000 | tf_op jit(solution)/shard_map/all_gather | solution.py:171
  14.0 5.1 %collective-permute-start = (bf16[1600,128]{1,0:T(8,128)(2,1)S(1)}, bf16[1600,128]{1,0:T(8,128)(2,1)S(1)}, u32[]{:S(2)}, u32[]{:S(2)}) collective-permute-start(bf16[1600,128]{1,0:T(8,128)(2,1)S(1)} %all_gather.3.refs_0_), channel_id=1, source_target_pairs={{0,64},{8,72},{16,80},{24,88},{32,96},{40,104},{48,112},{56,120},{... | collective-permute-start | bytes 1228808 | tf_op jit(solution)/shard_map/ppermute | solution.py:28
  19.1 12.2 %collective-permute-start.1 = (bf16[1600,128]{1,0:T(8,128)(2,1)S(1)}, bf16[1600,128]{1,0:T(8,128)(2,1)S(1)}, u32[]{:S(2)}, u32[]{:S(2)}) collective-permute-start(bf16[1600,128]{1,0:T(8,128)(2,1)S(1)} %all_gather.3.refs_0_), channel_id=1, source_target_pairs={{0,704},{8,712},{16,720},{24,728},{32,736},{40,744},{48,752},{56,7... | collective-permute-start | bytes 1228808 | tf_op jit(solution)/shard_map/ppermute | solution.py:28
  31.4 5.4 %collective-permute-done.refs_1_ = bf16[1600,128]{1,0:T(8,128)(2,1)S(1)} collective-permute-done((bf16[1600,128]{1,0:T(8,128)(2,1)S(1)}, bf16[1600,128]{1,0:T(8,128)(2,1)S(1)}, u32[]{:S(2)}, u32[]{:S(2)}) %collective-permute-start) | collective-permute-done | bytes 409632 | tf_op jit(solution)/shard_map/ppermute | solution.py:28
  36.7 1.9 %collective-permute-start.2 = (bf16[1600,128]{1,0:T(8,128)(2,1)S(1)}, bf16[1600,128]{1,0:T(8,128)(2,1)S(1)}, u32[]{:S(2)}, u32[]{:S(2)}) collective-permute-start(bf16[1600,128]{1,0:T(8,128)(2,1)S(1)} %collective-permute-done.refs_1_), channel_id=1, source_target_pairs={{0,64},{8,72},{16,80},{24,88},{32,96},{40,104},{48,112},{56,120},{... | collective-permute-start | bytes 1228808 | tf_op jit(solution)/shard_map/ppermute | solution.py:28
  38.7 4.6 %collective-permute-start.3 = (bf16[1600,128]{1,0:T(8,128)(2,1)S(1)}, bf16[1600,128]{1,0:T(8,128)(2,1)S(1)}, u32[]{:S(2)}, u32[]{:S(2)}) collective-permute-start(bf16[1600,128]{1,0:T(8,128)(2,1)S(1)} %collective-permute-done.1.refs_2_), channel_id=1, source_target_pairs={{0,704},{8,712},{16,720},{24,728},{32,736},{40,744},{48,752},{56,7... | collective-permute-start | bytes 1228808 | tf_op jit(solution)/shard_map/ppermute | solution.py:28
  43.3 4.4 %collective-permute-done.2.refs_3_ = bf16[1600,128]{1,0:T(8,128)(2,1)S(1)} collective-permute-done((bf16[1600,128]{1,0:T(8,128)(2,1)S(1)}, bf16[1600,128]{1,0:T(8,128)(2,1)S(1)}, u32[]{:S(2)}, u32[]{:S(2)}) %collective-permute-start.2) | collective-permute-done | bytes 409632 | tf_op jit(solution)/shard_map/ppermute | solution.py:28
  47.7 1.9 %collective-permute-start.4 = (bf16[1600,128]{1,0:T(8,128)(2,1)S(1)}, bf16[1600,128]{1,0:T(8,128)(2,1)S(1)}, u32[]{:S(2)}, u32[]{:S(2)}) collective-permute-start(bf16[1600,128]{1,0:T(8,128)(2,1)S(1)} %collective-permute-done.2.refs_3_), channel_id=1, source_target_pairs={{0,64},{8,72},{16,80},{24,88},{32,96},{40,104},{48,112},{56,120},{... | collective-permute-start | bytes 1228808 | tf_op jit(solution)/shard_map/ppermute | solution.py:28
  49.6 4.6 %collective-permute-start.5 = (bf16[1600,128]{1,0:T(8,128)(2,1)S(1)}, bf16[1600,128]{1,0:T(8,128)(2,1)S(1)}, u32[]{:S(2)}, u32[]{:S(2)}) collective-permute-start(bf16[1600,128]{1,0:T(8,128)(2,1)S(1)} %collective-permute-done.3.refs_4_), channel_id=1, source_target_pairs={{0,704},{8,712},{16,720},{24,728},{32,736},{40,744},{48,752},{56,7... | collective-permute-start | bytes 1228808 | tf_op jit(solution)/shard_map/ppermute | solution.py:28
  54.4 3.3 %collective-permute-done.4.refs_5_ = bf16[1600,128]{1,0:T(8,128)(2,1)S(1)} collective-permute-done((bf16[1600,128]{1,0:T(8,128)(2,1)S(1)}, bf16[1600,128]{1,0:T(8,128)(2,1)S(1)}, u32[]{:S(2)}, u32[]{:S(2)}) %collective-permute-start.4) | collective-permute-done | bytes 409632 | tf_op jit(solution)/shard_map/ppermute | solution.py:28
  57.6 1.9 %collective-permute-start.6 = (bf16[1600,128]{1,0:T(8,128)(2,1)S(1)}, bf16[1600,128]{1,0:T(8,128)(2,1)S(1)}, u32[]{:S(2)}, u32[]{:S(2)}) collective-permute-start(bf16[1600,128]{1,0:T(8,128)(2,1)S(1)} %collective-permute-done.4.refs_5_), channel_id=1, source_target_pairs={{0,64},{8,72},{16,80},{24,88},{32,96},{40,104},{48,112},{56,120},{... | collective-permute-start | bytes 1228808 | tf_op jit(solution)/shard_map/ppermute | solution.py:28
  59.5 4.6 %collective-permute-start.7 = (bf16[1600,128]{1,0:T(8,128)(2,1)S(1)}, bf16[1600,128]{1,0:T(8,128)(2,1)S(1)}, u32[]{:S(2)}, u32[]{:S(2)}) collective-permute-start(bf16[1600,128]{1,0:T(8,128)(2,1)S(1)} %collective-permute-done.5.refs_6_), channel_id=1, source_target_pairs={{0,704},{8,712},{16,720},{24,728},{32,736},{40,744},{48,752},{56,7... | collective-permute-start | bytes 1228808 | tf_op jit(solution)/shard_map/ppermute | solution.py:28
  64.2 7.6 %collective-permute-start.11 = (bf16[8000,128]{1,0:T(8,128)(2,1)S(1)}, bf16[8000,128]{1,0:T(8,128)(2,1)S(1)}, u32[]{:S(2)}, u32[]{:S(2)}) collective-permute-start(bf16[8000,128]{1,0:T(8,128)(2,1)S(1)} %constant_dynamic-update-slice_fusion), channel_id=1, source_target_pairs={{0,8},{8,0},{16,24},{24,16},{32,40},{40,32},{48,56},{56,48},{64,72... | collective-permute-start | bytes 6144008 | tf_op jit(solution)/shard_map/ppermute | solution.py:28
  71.9 1.9 %collective-permute-start.8 = (bf16[1600,128]{1,0:T(8,128)(2,1)S(1)}, bf16[1600,128]{1,0:T(8,128)(2,1)S(1)}, u32[]{:S(2)}, u32[]{:S(2)}) collective-permute-start(bf16[1600,128]{1,0:T(8,128)(2,1)S(1)} %collective-permute-done.6.refs_7_), channel_id=1, source_target_pairs={{0,64},{8,72},{16,80},{24,88},{32,96},{40,104},{48,112},{56,120},{... | collective-permute-start | bytes 1228808 | tf_op jit(solution)/shard_map/ppermute | solution.py:28
  73.8 4.6 %collective-permute-start.9 = (bf16[1600,128]{1,0:T(8,128)(2,1)S(1)}, bf16[1600,128]{1,0:T(8,128)(2,1)S(1)}, u32[]{:S(2)}, u32[]{:S(2)}) collective-permute-start(bf16[1600,128]{1,0:T(8,128)(2,1)S(1)} %collective-permute-done.7.refs_8_), channel_id=1, source_target_pairs={{0,704},{8,712},{16,720},{24,728},{32,736},{40,744},{48,752},{56,7... | collective-permute-start | bytes 1228808 | tf_op jit(solution)/shard_map/ppermute | solution.py:28
  78.4 0.1 pad_maximum_fusion
  78.5 4.5 %collective-permute-start.12 = (bf16[6400,128]{1,0:T(8,128)(2,1)S(1)}, bf16[6400,128]{1,0:T(8,128)(2,1)S(1)}, u32[]{:S(2)}, u32[]{:S(2)}) collective-permute-start(bf16[6400,128]{1,0:T(8,128)(2,1)S(1)} %pad_maximum_fusion), channel_id=1, source_target_pairs={{0,8},{8,0},{16,24},{24,16},{32,40},{40,32},{48,56},{56,48},{64,72... | collective-permute-start | bytes 4915208 | tf_op jit(solution)/shard_map/ppermute | solution.py:28
  83.1 1.0 collective-permute-done.8.refs_9_
  84.0 0.9 collective-permute-done.9.refs_10_
  85.0 5.3 %collective-permute-start.10 = (bf16[1600,128]{1,0:T(8,128)(2,1)S(1)}, bf16[1600,128]{1,0:T(8,128)(2,1)S(1)}, u32[]{:S(2)}, u32[]{:S(2)}) collective-permute-start(bf16[1600,128]{1,0:T(8,128)(2,1)S(1)} %broadcast_select_fusion), channel_id=1, source_target_pairs={{0,64},{8,712},{16,80},{24,728},{32,96},{40,744},{48,112},{56,760}... | collective-permute-start | bytes 1228808 | tf_op jit(solution)/shard_map/ppermute | solution.py:28
  90.4 1.9 %collective-permute-start.13 = (bf16[3200,128]{1,0:T(8,128)(2,1)S(1)}, bf16[3200,128]{1,0:T(8,128)(2,1)S(1)}, u32[]{:S(2)}, u32[]{:S(2)}) collective-permute-start(bf16[3200,128]{1,0:T(8,128)(2,1)S(1)} %pad_maximum_fusion.1), channel_id=1, source_target_pairs={{0,8},{8,0},{16,24},{24,16},{32,40},{40,32},{48,56},{56,48},{64,72... | collective-permute-start | bytes 2457608 | tf_op jit(solution)/shard_map/ppermute | solution.py:28
  92.3 2.9 %collective-permute-done.10.refs_11_ = bf16[1600,128]{1,0:T(8,128)(2,1)S(1)} collective-permute-done((bf16[1600,128]{1,0:T(8,128)(2,1)S(1)}, bf16[1600,128]{1,0:T(8,128)(2,1)S(1)}, u32[]{:S(2)}, u32[]{:S(2)}) %collective-permute-start.10) | collective-permute-done | bytes 409632 | tf_op jit(solution)/shard_map/ppermute | solution.py:28
  95.2 6.3 %collective-permute-start.14 = (bf16[1600,128]{1,0:T(8,128)(2,1)S(1)}, bf16[1600,128]{1,0:T(8,128)(2,1)S(1)}, u32[]{:S(2)}, u32[]{:S(2)}) collective-permute-start(bf16[1600,128]{1,0:T(8,128)(2,1)S(1)} %collective-permute-done.10.refs_11_), channel_id=1, source_target_pairs={{0,8},{8,0},{16,24},{24,16},{32,40},{40,32},{48,56},{56,48},{64,72... | collective-permute-start | bytes 1228808 | tf_op jit(solution)/shard_map/ppermute | solution.py:28
  101.5 1.4 collective-permute-done.14.refs_15_
  102.9 15.1 %shard_map.77 = (bf16[128,1792]{1,0:T(8,128)(2,1)}, bf16[8,128,448]{2,1,0:T(8,128)(2,1)S(1)}) custom-call(bf16[1600,128]{1,0:T(8,128)(2,1)S(1)} %all_gather.3.refs_0_, bf16[1600,128]{1,0:T(8,128)(2,1)S(1)} %collective-permute-done.refs_1_, bf16[1600,128]{1,0:T(8,128)(2,1)S(1)} %collective-permute-done.1.refs_2_, ...), custom_call_target="tpu_custom_call" | custom-call | flops 3288334336 | bytes 9830400 | tf_op jit(solution)/shard_map/pallas_call | solution.py:142
  118.0 0.6 copy.8
  118.7 31.7 %all_to_all.5 = bf16[8,128,448]{1,2,0:T(8,128)(2,1)S(1)} all-to-all(bf16[8,128,448]{1,2,0:T(8,128)(2,1)S(1)} %copy.8), channel_id=1, replica_groups=mesh['fsdp'=96,'tp'=8] {'tp'}, dimensions={0} | all-to-all | bytes 1835008 | tf_op jit(solution)/shard_map/all_to_all | solution.py:182
  150.4 0.8 reduce_sum.12
  (21 shorter events, 0.4 us)
Async XLA Ops:
  14.0 22.8 %collective-permute-start = (bf16[1600,128]{1,0:T(8,128)(2,1)S(1)}, bf16[1600,128]{1,0:T(8,128)(2,1)S(1)}, u32[]{:S(2)}, u32[]{:S(2)}) collective-permute-start(bf16[1600,128]{1,0:T(8,128)(2,1)S(1)} %all_gather.3.refs_0_), channel_id=1, source_target_pairs={{0,64},{8,72},{16,80},{24,88},{32,96},{40,104},{48,112},{56,120},{... | collective-permute-start | bytes 1228808 | tf_op jit(solution)/shard_map/ppermute | solution.py:28
  19.1 19.5 %collective-permute-start.1 = (bf16[1600,128]{1,0:T(8,128)(2,1)S(1)}, bf16[1600,128]{1,0:T(8,128)(2,1)S(1)}, u32[]{:S(2)}, u32[]{:S(2)}) collective-permute-start(bf16[1600,128]{1,0:T(8,128)(2,1)S(1)} %all_gather.3.refs_0_), channel_id=1, source_target_pairs={{0,704},{8,712},{16,720},{24,728},{32,736},{40,744},{48,752},{56,7... | collective-permute-start | bytes 1228808 | tf_op jit(solution)/shard_map/ppermute | solution.py:28
  36.7 11.0 %collective-permute-start.2 = (bf16[1600,128]{1,0:T(8,128)(2,1)S(1)}, bf16[1600,128]{1,0:T(8,128)(2,1)S(1)}, u32[]{:S(2)}, u32[]{:S(2)}) collective-permute-start(bf16[1600,128]{1,0:T(8,128)(2,1)S(1)} %collective-permute-done.refs_1_), channel_id=1, source_target_pairs={{0,64},{8,72},{16,80},{24,88},{32,96},{40,104},{48,112},{56,120},{... | collective-permute-start | bytes 1228808 | tf_op jit(solution)/shard_map/ppermute | solution.py:28
  38.7 11.0 %collective-permute-start.3 = (bf16[1600,128]{1,0:T(8,128)(2,1)S(1)}, bf16[1600,128]{1,0:T(8,128)(2,1)S(1)}, u32[]{:S(2)}, u32[]{:S(2)}) collective-permute-start(bf16[1600,128]{1,0:T(8,128)(2,1)S(1)} %collective-permute-done.1.refs_2_), channel_id=1, source_target_pairs={{0,704},{8,712},{16,720},{24,728},{32,736},{40,744},{48,752},{56,7... | collective-permute-start | bytes 1228808 | tf_op jit(solution)/shard_map/ppermute | solution.py:28
  47.7 9.9 %collective-permute-start.4 = (bf16[1600,128]{1,0:T(8,128)(2,1)S(1)}, bf16[1600,128]{1,0:T(8,128)(2,1)S(1)}, u32[]{:S(2)}, u32[]{:S(2)}) collective-permute-start(bf16[1600,128]{1,0:T(8,128)(2,1)S(1)} %collective-permute-done.2.refs_3_), channel_id=1, source_target_pairs={{0,64},{8,72},{16,80},{24,88},{32,96},{40,104},{48,112},{56,120},{... | collective-permute-start | bytes 1228808 | tf_op jit(solution)/shard_map/ppermute | solution.py:28
  49.6 9.9 %collective-permute-start.5 = (bf16[1600,128]{1,0:T(8,128)(2,1)S(1)}, bf16[1600,128]{1,0:T(8,128)(2,1)S(1)}, u32[]{:S(2)}, u32[]{:S(2)}) collective-permute-start(bf16[1600,128]{1,0:T(8,128)(2,1)S(1)} %collective-permute-done.3.refs_4_), channel_id=1, source_target_pairs={{0,704},{8,712},{16,720},{24,728},{32,736},{40,744},{48,752},{56,7... | collective-permute-start | bytes 1228808 | tf_op jit(solution)/shard_map/ppermute | solution.py:28
  57.6 14.3 %collective-permute-start.6 = (bf16[1600,128]{1,0:T(8,128)(2,1)S(1)}, bf16[1600,128]{1,0:T(8,128)(2,1)S(1)}, u32[]{:S(2)}, u32[]{:S(2)}) collective-permute-start(bf16[1600,128]{1,0:T(8,128)(2,1)S(1)} %collective-permute-done.4.refs_5_), channel_id=1, source_target_pairs={{0,64},{8,72},{16,80},{24,88},{32,96},{40,104},{48,112},{56,120},{... | collective-permute-start | bytes 1228808 | tf_op jit(solution)/shard_map/ppermute | solution.py:28
  59.5 14.3 %collective-permute-start.7 = (bf16[1600,128]{1,0:T(8,128)(2,1)S(1)}, bf16[1600,128]{1,0:T(8,128)(2,1)S(1)}, u32[]{:S(2)}, u32[]{:S(2)}) collective-permute-start(bf16[1600,128]{1,0:T(8,128)(2,1)S(1)} %collective-permute-done.5.refs_6_), channel_id=1, source_target_pairs={{0,704},{8,712},{16,720},{24,728},{32,736},{40,744},{48,752},{56,7... | collective-permute-start | bytes 1228808 | tf_op jit(solution)/shard_map/ppermute | solution.py:28
  64.2 38.6 %collective-permute-start.11 = (bf16[8000,128]{1,0:T(8,128)(2,1)S(1)}, bf16[8000,128]{1,0:T(8,128)(2,1)S(1)}, u32[]{:S(2)}, u32[]{:S(2)}) collective-permute-start(bf16[8000,128]{1,0:T(8,128)(2,1)S(1)} %constant_dynamic-update-slice_fusion), channel_id=1, source_target_pairs={{0,8},{8,0},{16,24},{24,16},{32,40},{40,32},{48,56},{56,48},{64,72... | collective-permute-start | bytes 6144008 | tf_op jit(solution)/shard_map/ppermute | solution.py:28
  71.9 12.1 %collective-permute-start.8 = (bf16[1600,128]{1,0:T(8,128)(2,1)S(1)}, bf16[1600,128]{1,0:T(8,128)(2,1)S(1)}, u32[]{:S(2)}, u32[]{:S(2)}) collective-permute-start(bf16[1600,128]{1,0:T(8,128)(2,1)S(1)} %collective-permute-done.6.refs_7_), channel_id=1, source_target_pairs={{0,64},{8,72},{16,80},{24,88},{32,96},{40,104},{48,112},{56,120},{... | collective-permute-start | bytes 1228808 | tf_op jit(solution)/shard_map/ppermute | solution.py:28
  73.8 11.1 %collective-permute-start.9 = (bf16[1600,128]{1,0:T(8,128)(2,1)S(1)}, bf16[1600,128]{1,0:T(8,128)(2,1)S(1)}, u32[]{:S(2)}, u32[]{:S(2)}) collective-permute-start(bf16[1600,128]{1,0:T(8,128)(2,1)S(1)} %collective-permute-done.7.refs_8_), channel_id=1, source_target_pairs={{0,704},{8,712},{16,720},{24,728},{32,736},{40,744},{48,752},{56,7... | collective-permute-start | bytes 1228808 | tf_op jit(solution)/shard_map/ppermute | solution.py:28
  78.5 24.4 %copy-start = (bf16[128,3584]{1,0:T(8,128)(2,1)S(1)}, bf16[128,3584]{1,0:T(8,128)(2,1)}, u32[]{:S(2)}) copy-start(bf16[128,3584]{1,0:T(8,128)(2,1)} %refs_16_.1) | copy-start | bytes 2752516
  78.5 24.4 %copy-start.1 = (bf16[128,1792]{1,0:T(8,128)(2,1)S(1)}, bf16[128,1792]{1,0:T(8,128)(2,1)}, u32[]{:S(2)}) copy-start(bf16[128,1792]{1,0:T(8,128)(2,1)} %refs_17_.1) | copy-start | bytes 1376260
  78.5 24.4 %collective-permute-start.12 = (bf16[6400,128]{1,0:T(8,128)(2,1)S(1)}, bf16[6400,128]{1,0:T(8,128)(2,1)S(1)}, u32[]{:S(2)}, u32[]{:S(2)}) collective-permute-start(bf16[6400,128]{1,0:T(8,128)(2,1)S(1)} %pad_maximum_fusion), channel_id=1, source_target_pairs={{0,8},{8,0},{16,24},{24,16},{32,40},{40,32},{48,56},{56,48},{64,72... | collective-permute-start | bytes 4915208 | tf_op jit(solution)/shard_map/ppermute | solution.py:28
  85.0 10.2 %collective-permute-start.10 = (bf16[1600,128]{1,0:T(8,128)(2,1)S(1)}, bf16[1600,128]{1,0:T(8,128)(2,1)S(1)}, u32[]{:S(2)}, u32[]{:S(2)}) collective-permute-start(bf16[1600,128]{1,0:T(8,128)(2,1)S(1)} %broadcast_select_fusion), channel_id=1, source_target_pairs={{0,64},{8,712},{16,80},{24,728},{32,96},{40,744},{48,112},{56,760}... | collective-permute-start | bytes 1228808 | tf_op jit(solution)/shard_map/ppermute | solution.py:28
  90.4 12.5 %collective-permute-start.13 = (bf16[3200,128]{1,0:T(8,128)(2,1)S(1)}, bf16[3200,128]{1,0:T(8,128)(2,1)S(1)}, u32[]{:S(2)}, u32[]{:S(2)}) collective-permute-start(bf16[3200,128]{1,0:T(8,128)(2,1)S(1)} %pad_maximum_fusion.1), channel_id=1, source_target_pairs={{0,8},{8,0},{16,24},{24,16},{32,40},{40,32},{48,56},{56,48},{64,72... | collective-permute-start | bytes 2457608 | tf_op jit(solution)/shard_map/ppermute | solution.py:28
  95.2 7.7 %collective-permute-start.14 = (bf16[1600,128]{1,0:T(8,128)(2,1)S(1)}, bf16[1600,128]{1,0:T(8,128)(2,1)S(1)}, u32[]{:S(2)}, u32[]{:S(2)}) collective-permute-start(bf16[1600,128]{1,0:T(8,128)(2,1)S(1)} %collective-permute-done.10.refs_11_), channel_id=1, source_target_pairs={{0,8},{8,0},{16,24},{24,16},{32,40},{40,32},{48,56},{56,48},{64,72... | collective-permute-start | bytes 1228808 | tf_op jit(solution)/shard_map/ppermute | solution.py:28

commit v3 on v2

v3 whole, which is shorter than its diff:
```python
import math

import jax
import jax.numpy as jnp
from jax import lax
from jax.experimental import pallas as pl
from jax.experimental.pallas import tpu as pltpu
from jax.sharding import PartitionSpec as P

gelu_scale = math.sqrt(2.0 / math.pi)

BLK = 128
CAP = 3
META = 16
UNIT = CAP * BLK + META
SPOT = 8
SPOTS = BLK // SPOT
NX = 4
NZ = 12
NC = 2
PLACES = [(z, x, c) for z in range(NZ) for x in range(NX) for c in range(NC)]


def place(z, x, c):
    return ((z % NZ) * NX + x % NX) * NC + c % NC


def shift(value, move):
    pairs = [(place(*p), place(*move(*p))) for p in PLACES]
    return lax.ppermute(value, "fsdp", pairs)


def up(value):
    return shift(value, lambda z, x, c: (z + 1, x, c))


def down(value):
    return shift(value, lambda z, x, c: (z - 1, x, c))


def apart(value):
    return shift(value, lambda z, x, c: (z + 1 - 2 * c, x, c))


def sibling(value):
    return shift(value, lambda z, x, c: (z, x, 1 - c))


def gelu_parts(preact):
    cube = preact * preact * preact
    tangent = jnp.tanh(gelu_scale * (preact + 0.044715 * cube))
    activated = 0.5 * preact * (1.0 + tangent)
    derivative = 0.5 * (1.0 + tangent) + 0.5 * preact * (1.0 - tangent * tangent) * gelu_scale * (
        1.0 + 3.0 * 0.044715 * preact * preact
    )
    return (activated, derivative)


def pack(w_blocks, blk_rows, blk_cols, counts):
    live = jnp.arange(CAP, dtype=jnp.int32) < counts.reshape(1)
    blocks = jnp.where(live[:, None, None], w_blocks.reshape(CAP, BLK, BLK), jnp.bfloat16(0))
    places = jnp.concatenate([blk_rows.reshape(1, CAP), blk_cols.reshape(1, CAP)], axis=1)
    owner = lax.axis_index("fsdp")
    meta = lax.dynamic_update_slice(
        jnp.zeros((META, BLK), jnp.bfloat16),
        places.astype(jnp.bfloat16),
        (owner // SPOTS, owner % SPOTS * SPOT),
    )
    return jnp.concatenate([blocks.reshape(CAP * BLK, BLK), meta], axis=0)


def read_places(sources, table, places, sem):
    total = jnp.zeros((META, BLK), jnp.float32)
    for source in sources:
        for first in range(0, source.shape[0], UNIT):
            total += source[first + CAP * BLK : first + UNIT, :].astype(jnp.float32)
    table[...] = total[:8].astype(jnp.int32)
    fetch = pltpu.make_async_copy(table, places, sem)
    fetch.start()
    return fetch


def place_of(move, x, s, places):
    dz, other = move
    me = lax.axis_index("fsdp")
    z = lax.shift_right_logical(me, 3) + dz
    z = jnp.where(z < 0, z + NZ, jnp.where(z >= NZ, z - NZ, z))
    owner = (z * NX + x) * NC + jnp.bitwise_xor(jnp.bitwise_and(me, 1), other)
    spot = lax.shift_right_logical(owner, 4)
    lane = jnp.bitwise_and(owner, SPOTS - 1) * SPOT + s
    return pl.multiple_of(places[spot, lane] * BLK, BLK), places[spot, lane + CAP]


def pair(dense, j, rows=slice(None)):
    return jnp.concatenate([dense[2 * j, rows, :], dense[2 * j + 1, rows, :]], axis=1)


def near_kernel(moves, *refs):
    n = len(moves)
    sources, tokens = refs[:n], refs[n]
    dense, preact, mark, table, places, sem = refs[1 + n :]
    fetch = read_places(sources, table, places, sem)
    columns, depth, _ = dense.shape

    def clear(i, _):
        at = pl.multiple_of(i * BLK, BLK)
        for j in range(columns):
            dense[j, pl.ds(at, BLK), :] = jnp.zeros((BLK, BLK), jnp.bfloat16)
        return 0

    lax.fori_loop(0, depth // BLK, clear, 0)
    fetch.wait()
    for source, rows in zip(sources, moves):
        for k, move in enumerate(rows):
            for x in range(NX):
                at = (k * NX + x) * UNIT
                spots = [place_of(move, x, s, places) for s in range(CAP)]
                blocks = [source[at + s * BLK : at + (s + 1) * BLK, :] for s in range(CAP)]
                for (row, col), block in zip(spots, blocks):
                    dense[col, pl.ds(row, BLK), :] = block
    for j in range(columns // 2):
        total = jnp.dot(tokens[...], pair(dense, j), preferred_element_type=jnp.float32)
        preact[2 * j], preact[2 * j + 1] = total[:, :BLK], total[:, BLK:]
    mark[...] = preact[0, :8, :]


def far_kernel(moves, *refs):
    n = len(moves)
    sources = refs[:n]
    tokens, cotangent, preact, _, hidden, pieces, dense = refs[n : 7 + n]
    table, places, dpre, extra, terms, sem = refs[7 + n :]
    fetch = read_places(sources, table, places, sem)
    extra[...] = jnp.zeros_like(extra)
    fetch.wait()
    blocks = [
        source[first + s * BLK : first + (s + 1) * BLK, :]
        for source in sources
        for first in range(0, source.shape[0], UNIT)
        for s in range(CAP)
    ]
    spots = [
        place_of(move, x, s, places)
        for rows in moves
        for move in rows
        for x in range(NX)
        for s in range(CAP)
    ]
    for i, (row, _) in enumerate(spots):
        terms[i] = jnp.dot(
            tokens[:, pl.ds(row, BLK)], blocks[i], preferred_element_type=jnp.float32
        )
    for i, (row, col) in enumerate(spots):
        dense[col, pl.ds(row, BLK), :] = blocks[i]
        extra[col] += terms[i]

    columns = dense.shape[0]
    for j in range(columns):
        here = slice(j * BLK, (j + 1) * BLK)
        activated, derivative = gelu_parts(preact[j] + extra[j])
        hidden[:, here] = activated.astype(jnp.bfloat16)
        dpre[:, here] = (cotangent[:, here].astype(jnp.float32) * derivative).astype(jnp.bfloat16)
    slab = pieces.shape[2]
    for d in range(pieces.shape[0]):
        total = jnp.zeros(pieces.shape[1:], jnp.float32)
        for j in range(columns // 2):
            total += lax.dot_general(
                dpre[:, 2 * j * BLK : 2 * (j + 1) * BLK],
                pair(dense, j, slice(d * slab, (d + 1) * slab)),
                (((1,), (1,)), ((), ())),
                preferred_element_type=jnp.float32,
            )
        pieces[d] = total.astype(jnp.bfloat16)


def specs(*spaces):
    return [pl.BlockSpec(memory_space=s) for s in spaces]


def near(moves, stacks, tokens, shard):
    n, units = len(stacks), sum(s.shape[0] for s in stacks) // UNIT
    stacks = [pltpu.with_memory_space_constraint(s, pltpu.VMEM) for s in stacks]
    rows, model_width = tokens.shape
    columns = shard // BLK
    return pl.pallas_call(
        lambda *refs: near_kernel(moves, *refs),
        out_shape=(
            pltpu.VMEM((columns, model_width, BLK), jnp.bfloat16),
            pltpu.VMEM((columns, rows, BLK), jnp.float32),
            jax.ShapeDtypeStruct((8, BLK), jnp.float32),
        ),
        in_specs=specs(*[pltpu.VMEM] * n, pltpu.VMEM),
        out_specs=specs(pltpu.VMEM, pltpu.VMEM, pltpu.VMEM),
        scratch_shapes=[
            pltpu.VMEM((8, BLK), jnp.int32),
            pltpu.SMEM((8, BLK), jnp.int32),
            pltpu.SemaphoreType.DMA,
        ],
        compiler_params=pltpu.CompilerParams(vmem_limit_bytes=8 * 1024 * 1024),
        cost_estimate=pl.CostEstimate(
            flops=2 * rows * model_width * shard,
            bytes_accessed=2 * units * UNIT * BLK + 4 * model_width * shard,
            transcendentals=0,
        ),
    )(*stacks, tokens)


def far(moves, stacks, tokens, cotangent, preact, dense, n_tp):
    n, units = len(stacks), sum(s.shape[0] for s in stacks) // UNIT
    stacks = [pltpu.with_memory_space_constraint(s, pltpu.VMEM) for s in stacks]
    rows, model_width = tokens.shape
    shard = cotangent.shape[1]
    hidden, pieces, _ = pl.pallas_call(
        lambda *refs: far_kernel(moves, *refs),
        out_shape=(
            jax.ShapeDtypeStruct((rows, shard), jnp.bfloat16),
            jax.ShapeDtypeStruct((n_tp, rows, model_width // n_tp), jnp.bfloat16),
            pltpu.VMEM(dense.shape, jnp.bfloat16),
        ),
        in_specs=specs(*[pltpu.VMEM] * n, *[pltpu.VMEM] * 4),
        out_specs=specs(pltpu.VMEM, pltpu.VMEM, pltpu.VMEM),
        input_output_aliases={n + 3: 2},
        scratch_shapes=[
            pltpu.VMEM((8, BLK), jnp.int32),
            pltpu.SMEM((8, BLK), jnp.int32),
            pltpu.VMEM((rows, shard), jnp.bfloat16),
            pltpu.VMEM(preact.shape, jnp.float32),
            pltpu.VMEM((units * CAP, rows, BLK), jnp.float32),
            pltpu.SemaphoreType.DMA,
        ],
        compiler_params=pltpu.CompilerParams(vmem_limit_bytes=8 * 1024 * 1024),
        cost_estimate=pl.CostEstimate(
            flops=2 * rows * model_width * shard,
            bytes_accessed=2 * units * UNIT * BLK + 2 * model_width * shard,
            transcendentals=rows * shard,
        ),
    )(*stacks, tokens, cotangent, preact, dense)
    return hidden, pieces


def after(value, mark):
    return pl.pallas_call(
        lambda *refs: None,
        out_shape=jax.ShapeDtypeStruct(value.shape, value.dtype),
        in_specs=specs(pl.ANY, pl.ANY),
        out_specs=pl.BlockSpec(memory_space=pl.ANY),
        input_output_aliases={0: 0},
        compiler_params=pltpu.CompilerParams(vmem_limit_bytes=1024 * 1024),
    )(value, mark)


def by_core_kernel(first, second, out, sem):
    core = jnp.bitwise_and(lax.axis_index("fsdp"), 1)

    @pl.when(core == 1)
    def _():
        copy = pltpu.make_async_copy(first, out, sem)
        copy.start()
        copy.wait()

    @pl.when(core == 0)
    def _():
        copy = pltpu.make_async_copy(second, out, sem)
        copy.start()
        copy.wait()


def by_core(first, second):
    return pl.pallas_call(
        by_core_kernel,
        out_shape=jax.ShapeDtypeStruct(first.shape, first.dtype),
        in_specs=specs(pl.ANY, pl.ANY),
        out_specs=pl.BlockSpec(memory_space=pl.ANY),
        scratch_shapes=[pltpu.SemaphoreType.DMA],
        compiler_params=pltpu.CompilerParams(vmem_limit_bytes=1024 * 1024),
    )(first, second)


def per_device(tokens, cotangent, w_blocks, blk_rows, blk_cols, counts):
    mine = pack(w_blocks, blk_rows, blk_cols, counts)
    by_x = [[place(z, x, c) for x in range(NX)] for z in range(NZ) for c in range(NC)]
    row = lax.all_gather(mine, "fsdp", axis=0, tiled=True, axis_index_groups=by_x)

    above, below = row, row
    held, moves = [row], [(0, 0)]
    for step in range(1, NZ // 2):
        above, below = up(above), down(below)
        held += [above, below]
        moves += [(-step, 0), (step, 0)]
    last = apart(by_core(below, above))
    stacks, rows = list(held), [[m] for m in moves]
    for part in (slice(0, 5), slice(5, 9), slice(9, 11)):
        stacks.append(sibling(jnp.concatenate(held[part], axis=0)))
        rows.append([(dz, 1) for dz, _ in moves[part]])
    dense, preact, mark = near(rows, stacks, tokens, cotangent.shape[1])
    last = after(last, mark)
    hidden, pieces = far(
        [[(NZ // 2, 0)], [(NZ // 2, 1)]],
        [last, sibling(last)],
        tokens,
        cotangent,
        preact,
        dense,
        lax.axis_size("tp"),
    )
    terms = lax.all_to_all(pieces, "tp", split_axis=0, concat_axis=0, tiled=True)
    summed = jnp.sum(terms.astype(jnp.float32), axis=0).astype(jnp.bfloat16)
    return (hidden, summed)


def solution(mesh):
    return jax.shard_map(
        per_device,
        mesh=mesh,
        in_specs=(
            P("fsdp", None),
            P("fsdp", "tp"),
            P("fsdp", "tp", None, None, None),
            P("fsdp", "tp", None),
            P("fsdp", "tp", None),
            P("fsdp", "tp"),
        ),
        out_specs=(P("fsdp", "tp"), P("fsdp", "tp")),
        check_vma=False,
    )
```

time: 152 us -> 145 us (0.954)
  Pallas kernels: 15.1 us -> 10.9 us
  waiting for transfers between devices: 19.2 us -> 16.3 us
    pallas_call x1 -> x4, Pallas kernels: 15.1 us -> 10.9 us  [the longest x1 5.43 us: far(): pl.pallas_call(lambda *refs: far_kernel(moves, *refs), out_shape=(jax.Sha...]
    ppermute x15, waiting for transfers between devices: 19.2 us -> 16.3 us  [shift(): return lax.ppermute(value, 'fsdp', pairs)]
  transfers between devices with their start and end apart: 15 -> 15, of which waited for: 7 -> 6; matrix products, arithmetic and copies ran while one was open for 0% -> 0% of each run, Pallas kernels for 0% -> 4%
where the time goes in v3:
time: 145 us; the launch traced here: 144 us
  starting transfers between devices  68.7 us (47%)
  blocking collectives  42.6 us (29%)
  waiting for transfers between devices  16.3 us (11%)
  Pallas kernels  10.9 us (8%)
  other arithmetic  2.72 us (2%)
  between operations  1.65 us (1%)
    ppermute x15, starting transfers between devices, shift(): return lax.ppermute(value, 'fsdp', pairs)  68.7 us
    all_to_all x1, blocking collectives, per_device(): lax.all_to_all(pieces, 'tp', split_axis=0, concat_axis=0, tiled=True)  31.8 us
    ppermute x15, waiting for transfers between devices, shift(): return lax.ppermute(value, 'fsdp', pairs)  16.3 us
    all_gather x1, blocking collectives, per_device(): lax.all_gather(mine, 'fsdp', axis=0, tiled=True, axis_index_groups=by_x)  10.8 us
    pallas_call x1, Pallas kernels, far(): pl.pallas_call(lambda *refs: far_kernel(moves, *refs), out_shape=(jax.Sha...  5.43 us
    pallas_call x1, Pallas kernels, near(): pl.pallas_call(lambda *refs: near_kernel(moves, *refs), out_shape=(pltpu....  5.2 us
  transfers between devices with their start and end apart: 15, of which 6 were waited for; matrix products, arithmetic and copies ran while one was open for 0% of the time, Pallas kernels for 4%

profile of v3, /device:TPU:1, one launch (start us, length us, event | category | flops | bytes accessed | tf_op | source)
XLA Modules:
  0.0 144.2 jit_solution(13168155074146368099)
XLA Ops:
  1.4 0.7 convert_bitcast_fusion
  2.1 1.0 bitcast_select_fusion
  3.2 0.3 dynamic_update_slice.3
  3.5 10.8 %all_gather.3.refs_0_ = bf16[1600,128]{1,0:T(8,128)(2,1)S(1)} all-gather(bf16[400,128]{1,0:T(8,128)(2,1)S(1)} %pad_maximum_fusion.2), channel_id=1, replica_groups={{0,16,32,48},{8,24,40,56},{64,80,96,112},{72,88,104,120},{128,144,160,1..., dimensions={0}, use_global_device_ids=true | all-gather | bytes 512000 | tf_op jit(solution)/shard_map/all_gather | solution.py:281
  14.3 5.1 %collective-permute-start.5 = (bf16[1600,128]{1,0:T(8,128)(2,1)S(1)}, bf16[1600,128]{1,0:T(8,128)(2,1)S(1)}, u32[]{:S(2)}, u32[]{:S(2)}) collective-permute-start(bf16[1600,128]{1,0:T(8,128)(2,1)S(1)} %all_gather.3.refs_0_), channel_id=1, source_target_pairs={{0,64},{8,72},{16,80},{24,88},{32,96},{40,104},{48,112},{56,120},{... | collective-permute-start | bytes 1228808 | tf_op jit(solution)/shard_map/ppermute | solution.py:30
  19.4 12.2 %collective-permute-start = (bf16[1600,128]{1,0:T(8,128)(2,1)S(1)}, bf16[1600,128]{1,0:T(8,128)(2,1)S(1)}, u32[]{:S(2)}, u32[]{:S(2)}) collective-permute-start(bf16[1600,128]{1,0:T(8,128)(2,1)S(1)} %all_gather.3.refs_0_), channel_id=1, source_target_pairs={{0,704},{8,712},{16,720},{24,728},{32,736},{40,744},{48,752},{56,7... | collective-permute-start | bytes 1228808 | tf_op jit(solution)/shard_map/ppermute | solution.py:30
  31.7 5.4 %collective-permute-done.5.refs_1_ = bf16[1600,128]{1,0:T(8,128)(2,1)S(1)} collective-permute-done((bf16[1600,128]{1,0:T(8,128)(2,1)S(1)}, bf16[1600,128]{1,0:T(8,128)(2,1)S(1)}, u32[]{:S(2)}, u32[]{:S(2)}) %collective-permute-start.5) | collective-permute-done | bytes 409632 | tf_op jit(solution)/shard_map/ppermute | solution.py:30
  37.1 1.9 %collective-permute-start.6 = (bf16[1600,128]{1,0:T(8,128)(2,1)S(1)}, bf16[1600,128]{1,0:T(8,128)(2,1)S(1)}, u32[]{:S(2)}, u32[]{:S(2)}) collective-permute-start(bf16[1600,128]{1,0:T(8,128)(2,1)S(1)} %collective-permute-done.5.refs_1_), channel_id=1, source_target_pairs={{0,64},{8,72},{16,80},{24,88},{32,96},{40,104},{48,112},{56,120},{... | collective-permute-start | bytes 1228808 | tf_op jit(solution)/shard_map/ppermute | solution.py:30
  39.0 4.6 %collective-permute-start.1 = (bf16[1600,128]{1,0:T(8,128)(2,1)S(1)}, bf16[1600,128]{1,0:T(8,128)(2,1)S(1)}, u32[]{:S(2)}, u32[]{:S(2)}) collective-permute-start(bf16[1600,128]{1,0:T(8,128)(2,1)S(1)} %collective-permute-done.refs_2_), channel_id=1, source_target_pairs={{0,704},{8,712},{16,720},{24,728},{32,736},{40,744},{48,752},{56,7... | collective-permute-start | bytes 1228808 | tf_op jit(solution)/shard_map/ppermute | solution.py:30
  43.6 4.4 %collective-permute-done.6.refs_3_ = bf16[1600,128]{1,0:T(8,128)(2,1)S(1)} collective-permute-done((bf16[1600,128]{1,0:T(8,128)(2,1)S(1)}, bf16[1600,128]{1,0:T(8,128)(2,1)S(1)}, u32[]{:S(2)}, u32[]{:S(2)}) %collective-permute-start.6) | collective-permute-done | bytes 409632 | tf_op jit(solution)/shard_map/ppermute | solution.py:30
  48.0 1.9 %collective-permute-start.7 = (bf16[1600,128]{1,0:T(8,128)(2,1)S(1)}, bf16[1600,128]{1,0:T(8,128)(2,1)S(1)}, u32[]{:S(2)}, u32[]{:S(2)}) collective-permute-start(bf16[1600,128]{1,0:T(8,128)(2,1)S(1)} %collective-permute-done.6.refs_3_), channel_id=1, source_target_pairs={{0,64},{8,72},{16,80},{24,88},{32,96},{40,104},{48,112},{56,120},{... | collective-permute-start | bytes 1228808 | tf_op jit(solution)/shard_map/ppermute | solution.py:30
  50.0 4.6 %collective-permute-start.2 = (bf16[1600,128]{1,0:T(8,128)(2,1)S(1)}, bf16[1600,128]{1,0:T(8,128)(2,1)S(1)}, u32[]{:S(2)}, u32[]{:S(2)}) collective-permute-start(bf16[1600,128]{1,0:T(8,128)(2,1)S(1)} %collective-permute-done.1.refs_4_), channel_id=1, source_target_pairs={{0,704},{8,712},{16,720},{24,728},{32,736},{40,744},{48,752},{56,7... | collective-permute-start | bytes 1228808 | tf_op jit(solution)/shard_map/ppermute | solution.py:30
  54.7 3.3 %collective-permute-done.7.refs_5_ = bf16[1600,128]{1,0:T(8,128)(2,1)S(1)} collective-permute-done((bf16[1600,128]{1,0:T(8,128)(2,1)S(1)}, bf16[1600,128]{1,0:T(8,128)(2,1)S(1)}, u32[]{:S(2)}, u32[]{:S(2)}) %collective-permute-start.7) | collective-permute-done | bytes 409632 | tf_op jit(solution)/shard_map/ppermute | solution.py:30
  57.9 1.9 %collective-permute-start.8 = (bf16[1600,128]{1,0:T(8,128)(2,1)S(1)}, bf16[1600,128]{1,0:T(8,128)(2,1)S(1)}, u32[]{:S(2)}, u32[]{:S(2)}) collective-permute-start(bf16[1600,128]{1,0:T(8,128)(2,1)S(1)} %collective-permute-done.7.refs_5_), channel_id=1, source_target_pairs={{0,64},{8,72},{16,80},{24,88},{32,96},{40,104},{48,112},{56,120},{... | collective-permute-start | bytes 1228808 | tf_op jit(solution)/shard_map/ppermute | solution.py:30
  59.9 4.6 %collective-permute-start.3 = (bf16[1600,128]{1,0:T(8,128)(2,1)S(1)}, bf16[1600,128]{1,0:T(8,128)(2,1)S(1)}, u32[]{:S(2)}, u32[]{:S(2)}) collective-permute-start(bf16[1600,128]{1,0:T(8,128)(2,1)S(1)} %collective-permute-done.2.refs_6_), channel_id=1, source_target_pairs={{0,704},{8,712},{16,720},{24,728},{32,736},{40,744},{48,752},{56,7... | collective-permute-start | bytes 1228808 | tf_op jit(solution)/shard_map/ppermute | solution.py:30
  64.6 7.6 %collective-permute-start.11 = (bf16[8000,128]{1,0:T(8,128)(2,1)S(1)}, bf16[8000,128]{1,0:T(8,128)(2,1)S(1)}, u32[]{:S(2)}, u32[]{:S(2)}) collective-permute-start(bf16[8000,128]{1,0:T(8,128)(2,1)S(1)} %constant_dynamic-update-slice_fusion), channel_id=1, source_target_pairs={{0,8},{8,0},{16,24},{24,16},{32,40},{40,32},{48,56},{56,48},{64,72... | collective-permute-start | bytes 6144008 | tf_op jit(solution)/shard_map/ppermute | solution.py:30
  72.2 1.9 %collective-permute-start.9 = (bf16[1600,128]{1,0:T(8,128)(2,1)S(1)}, bf16[1600,128]{1,0:T(8,128)(2,1)S(1)}, u32[]{:S(2)}, u32[]{:S(2)}) collective-permute-start(bf16[1600,128]{1,0:T(8,128)(2,1)S(1)} %collective-permute-done.8.refs_7_), channel_id=1, source_target_pairs={{0,64},{8,72},{16,80},{24,88},{32,96},{40,104},{48,112},{56,120},{... | collective-permute-start | bytes 1228808 | tf_op jit(solution)/shard_map/ppermute | solution.py:30
  74.1 4.6 %collective-permute-start.4 = (bf16[1600,128]{1,0:T(8,128)(2,1)S(1)}, bf16[1600,128]{1,0:T(8,128)(2,1)S(1)}, u32[]{:S(2)}, u32[]{:S(2)}) collective-permute-start(bf16[1600,128]{1,0:T(8,128)(2,1)S(1)} %collective-permute-done.3.refs_8_), channel_id=1, source_target_pairs={{0,704},{8,712},{16,720},{24,728},{32,736},{40,744},{48,752},{56,7... | collective-permute-start | bytes 1228808 | tf_op jit(solution)/shard_map/ppermute | solution.py:30
  78.7 0.1 pad_maximum_fusion
  78.9 4.5 %collective-permute-start.12 = (bf16[6400,128]{1,0:T(8,128)(2,1)S(1)}, bf16[6400,128]{1,0:T(8,128)(2,1)S(1)}, u32[]{:S(2)}, u32[]{:S(2)}) collective-permute-start(bf16[6400,128]{1,0:T(8,128)(2,1)S(1)} %pad_maximum_fusion), channel_id=1, source_target_pairs={{0,8},{8,0},{16,24},{24,16},{32,40},{40,32},{48,56},{56,48},{64,72... | collective-permute-start | bytes 4915208 | tf_op jit(solution)/shard_map/ppermute | solution.py:30
  83.4 1.0 collective-permute-done.9.second.refs_9_
  84.4 0.9 collective-permute-done.4.first.refs_10_
  85.3 5.0 %collective-permute-start.13 = (bf16[3200,128]{1,0:T(8,128)(2,1)S(1)}, bf16[3200,128]{1,0:T(8,128)(2,1)S(1)}, u32[]{:S(2)}, u32[]{:S(2)}) collective-permute-start(bf16[3200,128]{1,0:T(8,128)(2,1)S(1)} %pad_maximum_fusion.1), channel_id=1, source_target_pairs={{0,8},{8,0},{16,24},{24,16},{32,40},{40,32},{48,56},{56,48},{64,72... | collective-permute-start | bytes 2457608 | tf_op jit(solution)/shard_map/ppermute | solution.py:30
  90.4 0.2 shard_map.77
  90.6 5.5 %collective-permute-start.10 = (bf16[1600,128]{1,0:T(8,128)(2,1)S(1)}, bf16[1600,128]{1,0:T(8,128)(2,1)S(1)}, u32[]{:S(2)}, u32[]{:S(2)}) collective-permute-start(bf16[1600,128]{1,0:T(8,128)(2,1)S(1)} %shard_map.77), channel_id=1, source_target_pairs={{0,64},{8,712},{16,80},{24,728},{32,96},{40,744},{48,112},{56,760}... | collective-permute-start | bytes 1228808 | tf_op jit(solution)/shard_map/ppermute | solution.py:30
  96.1 5.2 %shard_map.78 = (bf16[14,3584,128]{2,1,0:T(8,128)(2,1)S(1)}, f32[14,128,128]{2,1,0:T(8,128)S(1)}, f32[8,128]{1,0:T(8,128)S(1)}) custom-call(bf16[1600,128]{1,0:T(8,128)(2,1)S(1)} %all_gather.3.refs_0_, bf16[1600,128]{1,0:T(8,128)(2,1)S(1)} %collective-permute-done.5.refs_1_, bf16[1600,128]{1,0:T(8,128)(2,1)S(1)} %collective-permute-done.refs_2_, ...), custom_call_target="tpu_custom_call" | custom-call | flops 1644167168 | bytes 34701312 | tf_op jit(solution)/shard_map/pallas_call | solution.py:184
  101.4 2.8 %collective-permute-start.14 = (bf16[1600,128]{1,0:T(8,128)(2,1)S(1)}, bf16[1600,128]{1,0:T(8,128)(2,1)S(1)}, u32[]{:S(2)}, u32[]{:S(2)}) collective-permute-start(bf16[1600,128]{1,0:T(8,128)(2,1)S(1)} %shard_map.79.refs_0_), channel_id=1, source_target_pairs={{0,8},{8,0},{16,24},{24,16},{32,40},{40,32},{48,56},{56,48},{64,72... | collective-permute-start | bytes 1228808 | tf_op jit(solution)/shard_map/ppermute | solution.py:30
  104.2 1.4 collective-permute-done.14.refs_1_
  105.6 5.4 %shard_map.80 = (bf16[128,1792]{1,0:T(8,128)(2,1)}, bf16[8,128,448]{2,1,0:T(8,128)(2,1)S(1)}, bf16[14,3584,128]{2,1,0:T(8,128)(2,1)S(1)}) custom-call(bf16[1600,128]{1,0:T(8,128)(2,1)S(1)} %shard_map.79.refs_0_, bf16[1600,128]{1,0:T(8,128)(2,1)S(1)} %collective-permute-done.14.refs_1_, ...), custom_call_target="tpu_custom_call", output_to_operand_aliasing={{2}: (5, {})} | custom-call | flops 1644167168 | bytes 13664256 | tf_op jit(solution)/shard_map/pallas_call | solution.py:212
  111.0 0.6 copy.10
  111.6 31.8 %all_to_all.5 = bf16[8,128,448]{1,2,0:T(8,128)(2,1)S(1)} all-to-all(bf16[8,128,448]{1,2,0:T(8,128)(2,1)S(1)} %copy.10), channel_id=1, replica_groups=mesh['fsdp'=96,'tp'=8] {'tp'}, dimensions={0} | all-to-all | bytes 1835008 | tf_op jit(solution)/shard_map/all_to_all | solution.py:305
  143.4 0.8 reduce_sum.12
  (25 shorter events, 0.5 us)
Async XLA Ops:
  14.3 22.8 %collective-permute-start.5 = (bf16[1600,128]{1,0:T(8,128)(2,1)S(1)}, bf16[1600,128]{1,0:T(8,128)(2,1)S(1)}, u32[]{:S(2)}, u32[]{:S(2)}) collective-permute-start(bf16[1600,128]{1,0:T(8,128)(2,1)S(1)} %all_gather.3.refs_0_), channel_id=1, source_target_pairs={{0,64},{8,72},{16,80},{24,88},{32,96},{40,104},{48,112},{56,120},{... | collective-permute-start | bytes 1228808 | tf_op jit(solution)/shard_map/ppermute | solution.py:30
  19.4 19.5 %collective-permute-start = (bf16[1600,128]{1,0:T(8,128)(2,1)S(1)}, bf16[1600,128]{1,0:T(8,128)(2,1)S(1)}, u32[]{:S(2)}, u32[]{:S(2)}) collective-permute-start(bf16[1600,128]{1,0:T(8,128)(2,1)S(1)} %all_gather.3.refs_0_), channel_id=1, source_target_pairs={{0,704},{8,712},{16,720},{24,728},{32,736},{40,744},{48,752},{56,7... | collective-permute-start | bytes 1228808 | tf_op jit(solution)/shard_map/ppermute | solution.py:30
  37.1 11.0 %collective-permute-start.6 = (bf16[1600,128]{1,0:T(8,128)(2,1)S(1)}, bf16[1600,128]{1,0:T(8,128)(2,1)S(1)}, u32[]{:S(2)}, u32[]{:S(2)}) collective-permute-start(bf16[1600,128]{1,0:T(8,128)(2,1)S(1)} %collective-permute-done.5.refs_1_), channel_id=1, source_target_pairs={{0,64},{8,72},{16,80},{24,88},{32,96},{40,104},{48,112},{56,120},{... | collective-permute-start | bytes 1228808 | tf_op jit(solution)/shard_map/ppermute | solution.py:30
  39.0 11.0 %collective-permute-start.1 = (bf16[1600,128]{1,0:T(8,128)(2,1)S(1)}, bf16[1600,128]{1,0:T(8,128)(2,1)S(1)}, u32[]{:S(2)}, u32[]{:S(2)}) collective-permute-start(bf16[1600,128]{1,0:T(8,128)(2,1)S(1)} %collective-permute-done.refs_2_), channel_id=1, source_target_pairs={{0,704},{8,712},{16,720},{24,728},{32,736},{40,744},{48,752},{56,7... | collective-permute-start | bytes 1228808 | tf_op jit(solution)/shard_map/ppermute | solution.py:30
  48.0 9.9 %collective-permute-start.7 = (bf16[1600,128]{1,0:T(8,128)(2,1)S(1)}, bf16[1600,128]{1,0:T(8,128)(2,1)S(1)}, u32[]{:S(2)}, u32[]{:S(2)}) collective-permute-start(bf16[1600,128]{1,0:T(8,128)(2,1)S(1)} %collective-permute-done.6.refs_3_), channel_id=1, source_target_pairs={{0,64},{8,72},{16,80},{24,88},{32,96},{40,104},{48,112},{56,120},{... | collective-permute-start | bytes 1228808 | tf_op jit(solution)/shard_map/ppermute | solution.py:30
  50.0 9.9 %collective-permute-start.2 = (bf16[1600,128]{1,0:T(8,128)(2,1)S(1)}, bf16[1600,128]{1,0:T(8,128)(2,1)S(1)}, u32[]{:S(2)}, u32[]{:S(2)}) collective-permute-start(bf16[1600,128]{1,0:T(8,128)(2,1)S(1)} %collective-permute-done.1.refs_4_), channel_id=1, source_target_pairs={{0,704},{8,712},{16,720},{24,728},{32,736},{40,744},{48,752},{56,7... | collective-permute-start | bytes 1228808 | tf_op jit(solution)/shard_map/ppermute | solution.py:30
  57.9 14.3 %collective-permute-start.8 = (bf16[1600,128]{1,0:T(8,128)(2,1)S(1)}, bf16[1600,128]{1,0:T(8,128)(2,1)S(1)}, u32[]{:S(2)}, u32[]{:S(2)}) collective-permute-start(bf16[1600,128]{1,0:T(8,128)(2,1)S(1)} %collective-permute-done.7.refs_5_), channel_id=1, source_target_pairs={{0,64},{8,72},{16,80},{24,88},{32,96},{40,104},{48,112},{56,120},{... | collective-permute-start | bytes 1228808 | tf_op jit(solution)/shard_map/ppermute | solution.py:30
  59.9 14.3 %collective-permute-start.3 = (bf16[1600,128]{1,0:T(8,128)(2,1)S(1)}, bf16[1600,128]{1,0:T(8,128)(2,1)S(1)}, u32[]{:S(2)}, u32[]{:S(2)}) collective-permute-start(bf16[1600,128]{1,0:T(8,128)(2,1)S(1)} %collective-permute-done.2.refs_6_), channel_id=1, source_target_pairs={{0,704},{8,712},{16,720},{24,728},{32,736},{40,744},{48,752},{56,7... | collective-permute-start | bytes 1228808 | tf_op jit(solution)/shard_map/ppermute | solution.py:30
  64.6 31.5 %collective-permute-start.11 = (bf16[8000,128]{1,0:T(8,128)(2,1)S(1)}, bf16[8000,128]{1,0:T(8,128)(2,1)S(1)}, u32[]{:S(2)}, u32[]{:S(2)}) collective-permute-start(bf16[8000,128]{1,0:T(8,128)(2,1)S(1)} %constant_dynamic-update-slice_fusion), channel_id=1, source_target_pairs={{0,8},{8,0},{16,24},{24,16},{32,40},{40,32},{48,56},{56,48},{64,72... | collective-permute-start | bytes 6144008 | tf_op jit(solution)/shard_map/ppermute | solution.py:30
  72.2 12.1 %collective-permute-start.9 = (bf16[1600,128]{1,0:T(8,128)(2,1)S(1)}, bf16[1600,128]{1,0:T(8,128)(2,1)S(1)}, u32[]{:S(2)}, u32[]{:S(2)}) collective-permute-start(bf16[1600,128]{1,0:T(8,128)(2,1)S(1)} %collective-permute-done.8.refs_7_), channel_id=1, source_target_pairs={{0,64},{8,72},{16,80},{24,88},{32,96},{40,104},{48,112},{56,120},{... | collective-permute-start | bytes 1228808 | tf_op jit(solution)/shard_map/ppermute | solution.py:30
  74.1 11.1 %collective-permute-start.4 = (bf16[1600,128]{1,0:T(8,128)(2,1)S(1)}, bf16[1600,128]{1,0:T(8,128)(2,1)S(1)}, u32[]{:S(2)}, u32[]{:S(2)}) collective-permute-start(bf16[1600,128]{1,0:T(8,128)(2,1)S(1)} %collective-permute-done.3.refs_8_), channel_id=1, source_target_pairs={{0,704},{8,712},{16,720},{24,728},{32,736},{40,744},{48,752},{56,7... | collective-permute-start | bytes 1228808 | tf_op jit(solution)/shard_map/ppermute | solution.py:30
  78.8 17.3 %copy-start = (bf16[128,3584]{1,0:T(8,128)(2,1)S(1)}, bf16[128,3584]{1,0:T(8,128)(2,1)}, u32[]{:S(2)}) copy-start(bf16[128,3584]{1,0:T(8,128)(2,1)} %refs_2_.1) | copy-start | bytes 2752516
  78.9 17.2 %collective-permute-start.12 = (bf16[6400,128]{1,0:T(8,128)(2,1)S(1)}, bf16[6400,128]{1,0:T(8,128)(2,1)S(1)}, u32[]{:S(2)}, u32[]{:S(2)}) collective-permute-start(bf16[6400,128]{1,0:T(8,128)(2,1)S(1)} %pad_maximum_fusion), channel_id=1, source_target_pairs={{0,8},{8,0},{16,24},{24,16},{32,40},{40,32},{48,56},{56,48},{64,72... | collective-permute-start | bytes 4915208 | tf_op jit(solution)/shard_map/ppermute | solution.py:30
  85.3 10.8 %collective-permute-start.13 = (bf16[3200,128]{1,0:T(8,128)(2,1)S(1)}, bf16[3200,128]{1,0:T(8,128)(2,1)S(1)}, u32[]{:S(2)}, u32[]{:S(2)}) collective-permute-start(bf16[3200,128]{1,0:T(8,128)(2,1)S(1)} %pad_maximum_fusion.1), channel_id=1, source_target_pairs={{0,8},{8,0},{16,24},{24,16},{32,40},{40,32},{48,56},{56,48},{64,72... | collective-permute-start | bytes 2457608 | tf_op jit(solution)/shard_map/ppermute | solution.py:30
  90.6 14.9 %copy-start.1 = (bf16[128,1792]{1,0:T(8,128)(2,1)S(1)}, bf16[128,1792]{1,0:T(8,128)(2,1)}, u32[]{:S(2)}) copy-start(bf16[128,1792]{1,0:T(8,128)(2,1)} %refs_3_.1) | copy-start | bytes 1376260
  90.6 10.7 %collective-permute-start.10 = (bf16[1600,128]{1,0:T(8,128)(2,1)S(1)}, bf16[1600,128]{1,0:T(8,128)(2,1)S(1)}, u32[]{:S(2)}, u32[]{:S(2)}) collective-permute-start(bf16[1600,128]{1,0:T(8,128)(2,1)S(1)} %shard_map.77), channel_id=1, source_target_pairs={{0,64},{8,712},{16,80},{24,728},{32,96},{40,744},{48,112},{56,760}... | collective-permute-start | bytes 1228808 | tf_op jit(solution)/shard_map/ppermute | solution.py:30
  101.4 4.2 %collective-permute-start.14 = (bf16[1600,128]{1,0:T(8,128)(2,1)S(1)}, bf16[1600,128]{1,0:T(8,128)(2,1)S(1)}, u32[]{:S(2)}, u32[]{:S(2)}) collective-permute-start(bf16[1600,128]{1,0:T(8,128)(2,1)S(1)} %shard_map.79.refs_0_), channel_id=1, source_target_pairs={{0,8},{8,0},{16,24},{24,16},{32,40},{40,32},{48,56},{56,48},{64,72... | collective-permute-start | bytes 1228808 | tf_op jit(solution)/shard_map/ppermute | solution.py:30

commit v4 on v3

--- a/solution.py
+++ b/solution.py
@@ -56,17 +56,37 @@
     return (activated, derivative)
 
 
+def pack_kernel(blocks, rows, cols, counts, out):
+    owner = lax.axis_index("fsdp")
+    for s in range(CAP):
+        here = slice(s * BLK, (s + 1) * BLK)
+
+        @pl.when(s < counts[0, 0])
+        def _(s=s, here=here):
+            out[here, :] = blocks[0, 0, s]
+
+        @pl.when(s >= counts[0, 0])
+        def _(here=here):
+            out[here, :] = jnp.zeros((BLK, BLK), jnp.bfloat16)
+
+    row = lax.broadcasted_iota(jnp.int32, (META, BLK), 0) - lax.shift_right_logical(owner, 4)
+    lane = lax.broadcasted_iota(jnp.int32, (META, BLK), 1)
+    lane = lane - jnp.bitwise_and(owner, SPOTS - 1) * SPOT
+    meta = jnp.zeros((META, BLK), jnp.float32)
+    for s in range(CAP):
+        for place, at in ((rows[0, 0, s], s), (cols[0, 0, s], s + CAP)):
+            meta = jnp.where((row == 0) & (lane == at), place.astype(jnp.float32), meta)
+    out[CAP * BLK :, :] = meta.astype(jnp.bfloat16)
+
+
 def pack(w_blocks, blk_rows, blk_cols, counts):
-    live = jnp.arange(CAP, dtype=jnp.int32) < counts.reshape(1)
-    blocks = jnp.where(live[:, None, None], w_blocks.reshape(CAP, BLK, BLK), jnp.bfloat16(0))
-    places = jnp.concatenate([blk_rows.reshape(1, CAP), blk_cols.reshape(1, CAP)], axis=1)
-    owner = lax.axis_index("fsdp")
-    meta = lax.dynamic_update_slice(
-        jnp.zeros((META, BLK), jnp.bfloat16),
-        places.astype(jnp.bfloat16),
-        (owner // SPOTS, owner % SPOTS * SPOT),
-    )
-    return jnp.concatenate([blocks.reshape(CAP * BLK, BLK), meta], axis=0)
+    return pl.pallas_call(
+        pack_kernel,
+        out_shape=jax.ShapeDtypeStruct((UNIT, BLK), jnp.bfloat16),
+        in_specs=specs(pltpu.VMEM, pltpu.SMEM, pltpu.SMEM, pltpu.SMEM),
+        out_specs=pl.BlockSpec(memory_space=pltpu.VMEM),
+        compiler_params=pltpu.CompilerParams(vmem_limit_bytes=4 * 1024 * 1024),
+    )(w_blocks, blk_rows, blk_cols, counts)
 
 
 def read_places(sources, table, places, sem):
@@ -159,13 +179,13 @@
         activated, derivative = gelu_parts(preact[j] + extra[j])
         hidden[:, here] = activated.astype(jnp.bfloat16)
         dpre[:, here] = (cotangent[:, here].astype(jnp.float32) * derivative).astype(jnp.bfloat16)
-    slab = pieces.shape[2]
+    slab = pieces.shape[1]
     for d in range(pieces.shape[0]):
         total = jnp.zeros(pieces.shape[1:], jnp.float32)
         for j in range(columns // 2):
             total += lax.dot_general(
+                pair(dense, j, slice(d * slab, (d + 1) * slab)),
                 dpre[:, 2 * j * BLK : 2 * (j + 1) * BLK],
-                pair(dense, j, slice(d * slab, (d + 1) * slab)),
                 (((1,), (1,)), ((), ())),
                 preferred_element_type=jnp.float32,
             )
@@ -213,7 +233,7 @@
         lambda *refs: far_kernel(moves, *refs),
         out_shape=(
             jax.ShapeDtypeStruct((rows, shard), jnp.bfloat16),
-            jax.ShapeDtypeStruct((n_tp, rows, model_width // n_tp), jnp.bfloat16),
+            jax.ShapeDtypeStruct((n_tp, model_width // n_tp, rows), jnp.bfloat16),
             pltpu.VMEM(dense.shape, jnp.bfloat16),
         ),
         in_specs=specs(*[pltpu.VMEM] * n, *[pltpu.VMEM] * 4),
@@ -248,7 +268,7 @@
     )(value, mark)
 
 
-def by_core_kernel(first, second, out, sem):
+def by_core_kernel(first, second, out, _first, _second, sem):
     core = jnp.bitwise_and(lax.axis_index("fsdp"), 1)
 
     @pl.when(core == 1)
@@ -267,9 +287,10 @@
 def by_core(first, second):
     return pl.pallas_call(
         by_core_kernel,
-        out_shape=jax.ShapeDtypeStruct(first.shape, first.dtype),
+        out_shape=(jax.ShapeDtypeStruct(first.shape, first.dtype),) * 3,
         in_specs=specs(pl.ANY, pl.ANY),
-        out_specs=pl.BlockSpec(memory_space=pl.ANY),
+        out_specs=specs(pl.ANY, pl.ANY, pl.ANY),
+        input_output_aliases={0: 1, 1: 2},
         scratch_shapes=[pltpu.SemaphoreType.DMA],
         compiler_params=pltpu.CompilerParams(vmem_limit_bytes=1024 * 1024),
     )(first, second)
@@ -286,7 +307,9 @@
         above, below = up(above), down(below)
         held += [above, below]
         moves += [(-step, 0), (step, 0)]
-    last = apart(by_core(below, above))
+    chosen, below, above = by_core(below, above)
+    last = apart(chosen)
+    held[-2:] = [above, below]
     stacks, rows = list(held), [[m] for m in moves]
     for part in (slice(0, 5), slice(5, 9), slice(9, 11)):
         stacks.append(sibling(jnp.concatenate(held[part], axis=0)))
@@ -304,7 +327,7 @@
     )
     terms = lax.all_to_all(pieces, "tp", split_axis=0, concat_axis=0, tiled=True)
     summed = jnp.sum(terms.astype(jnp.float32), axis=0).astype(jnp.bfloat16)
-    return (hidden, summed)
+    return (hidden, summed.T)
 
 
 def solution(mesh):

time: 145 us -> 144 us (level)
  other arithmetic: 2.72 us -> 0.94 us
    unnamed x8 -> x14, local copies, waits for them, and re-layouts: 0.21 us -> 2.4 us
where the time goes in v4:
time: 144 us
  starting transfers between devices  68.7 us (48%)
  blocking collectives  42.6 us (30%)
  waiting for transfers between devices  16.3 us (11%)
  Pallas kernels  10.8 us (8%)
  local copies, waits for them, and re-layouts  2.46 us (2%)
  between operations  1.6 us (1%)
    ppermute x15, starting transfers between devices, shift(): return lax.ppermute(value, 'fsdp', pairs)  68.7 us
    all_to_all x1, blocking collectives, per_device(): lax.all_to_all(pieces, 'tp', split_axis=0, concat_axis=0, tiled=True)  31.8 us
    ppermute x15, waiting for transfers between devices, shift(): return lax.ppermute(value, 'fsdp', pairs)  16.3 us
    all_gather x1, blocking collectives, per_device(): lax.all_gather(mine, 'fsdp', axis=0, tiled=True, axis_index_groups=by_x)  10.8 us
    pallas_call x1, Pallas kernels, near(): pl.pallas_call(lambda *refs: near_kernel(moves, *refs), out_shape=(pltpu....  5.2 us
    pallas_call x1, Pallas kernels, far(): pl.pallas_call(lambda *refs: far_kernel(moves, *refs), out_shape=(jax.Sha...  4.81 us
  transfers between devices with their start and end apart: 15, of which 6 were waited for; matrix products, arithmetic and copies ran while one was open for 0% of the time, Pallas kernels for 4%

profile of v4, /device:TPU:1, one launch (start us, length us, event | category | flops | bytes accessed | tf_op | source)
XLA Modules:
  0.0 143.5 jit_solution(6828943565728125479)
XLA Ops:
  1.3 0.9 copy-done.2
  2.2 0.7 copy-done.3
  2.8 0.7 copy-done.4
  3.5 0.6 shard_map.77
  4.1 10.8 %all_gather.3.refs_0_ = bf16[1600,128]{1,0:T(8,128)(2,1)S(1)} all-gather(bf16[400,128]{1,0:T(8,128)(2,1)S(1)} %shard_map.77), channel_id=1, replica_groups={{0,16,32,48},{8,24,40,56},{64,80,96,112},{72,88,104,120},{128,144,160,1..., dimensions={0}, use_global_device_ids=true | all-gather | bytes 512000 | tf_op jit(solution)/shard_map/all_gather | solution.py:302
  14.9 5.1 %collective-permute-start.5 = (bf16[1600,128]{1,0:T(8,128)(2,1)S(1)}, bf16[1600,128]{1,0:T(8,128)(2,1)S(1)}, u32[]{:S(2)}, u32[]{:S(2)}) collective-permute-start(bf16[1600,128]{1,0:T(8,128)(2,1)S(1)} %all_gather.3.refs_0_), channel_id=1, source_target_pairs={{0,64},{8,72},{16,80},{24,88},{32,96},{40,104},{48,112},{56,120},{... | collective-permute-start | bytes 1228808 | tf_op jit(solution)/shard_map/ppermute | solution.py:30
  20.1 12.2 %collective-permute-start = (bf16[1600,128]{1,0:T(8,128)(2,1)S(1)}, bf16[1600,128]{1,0:T(8,128)(2,1)S(1)}, u32[]{:S(2)}, u32[]{:S(2)}) collective-permute-start(bf16[1600,128]{1,0:T(8,128)(2,1)S(1)} %all_gather.3.refs_0_), channel_id=1, source_target_pairs={{0,704},{8,712},{16,720},{24,728},{32,736},{40,744},{48,752},{56,7... | collective-permute-start | bytes 1228808 | tf_op jit(solution)/shard_map/ppermute | solution.py:30
  32.3 5.4 %collective-permute-done.5.refs_1_ = bf16[1600,128]{1,0:T(8,128)(2,1)S(1)} collective-permute-done((bf16[1600,128]{1,0:T(8,128)(2,1)S(1)}, bf16[1600,128]{1,0:T(8,128)(2,1)S(1)}, u32[]{:S(2)}, u32[]{:S(2)}) %collective-permute-start.5) | collective-permute-done | bytes 409632 | tf_op jit(solution)/shard_map/ppermute | solution.py:30
  37.7 1.9 %collective-permute-start.6 = (bf16[1600,128]{1,0:T(8,128)(2,1)S(1)}, bf16[1600,128]{1,0:T(8,128)(2,1)S(1)}, u32[]{:S(2)}, u32[]{:S(2)}) collective-permute-start(bf16[1600,128]{1,0:T(8,128)(2,1)S(1)} %collective-permute-done.5.refs_1_), channel_id=1, source_target_pairs={{0,64},{8,72},{16,80},{24,88},{32,96},{40,104},{48,112},{56,120},{... | collective-permute-start | bytes 1228808 | tf_op jit(solution)/shard_map/ppermute | solution.py:30
  39.6 4.6 %collective-permute-start.1 = (bf16[1600,128]{1,0:T(8,128)(2,1)S(1)}, bf16[1600,128]{1,0:T(8,128)(2,1)S(1)}, u32[]{:S(2)}, u32[]{:S(2)}) collective-permute-start(bf16[1600,128]{1,0:T(8,128)(2,1)S(1)} %collective-permute-done.refs_2_), channel_id=1, source_target_pairs={{0,704},{8,712},{16,720},{24,728},{32,736},{40,744},{48,752},{56,7... | collective-permute-start | bytes 1228808 | tf_op jit(solution)/shard_map/ppermute | solution.py:30
  44.2 4.4 %collective-permute-done.6.refs_3_ = bf16[1600,128]{1,0:T(8,128)(2,1)S(1)} collective-permute-done((bf16[1600,128]{1,0:T(8,128)(2,1)S(1)}, bf16[1600,128]{1,0:T(8,128)(2,1)S(1)}, u32[]{:S(2)}, u32[]{:S(2)}) %collective-permute-start.6) | collective-permute-done | bytes 409632 | tf_op jit(solution)/shard_map/ppermute | solution.py:30
  48.7 1.9 %collective-permute-start.7 = (bf16[1600,128]{1,0:T(8,128)(2,1)S(1)}, bf16[1600,128]{1,0:T(8,128)(2,1)S(1)}, u32[]{:S(2)}, u32[]{:S(2)}) collective-permute-start(bf16[1600,128]{1,0:T(8,128)(2,1)S(1)} %collective-permute-done.6.refs_3_), channel_id=1, source_target_pairs={{0,64},{8,72},{16,80},{24,88},{32,96},{40,104},{48,112},{56,120},{... | collective-permute-start | bytes 1228808 | tf_op jit(solution)/shard_map/ppermute | solution.py:30
  50.6 4.6 %collective-permute-start.2 = (bf16[1600,128]{1,0:T(8,128)(2,1)S(1)}, bf16[1600,128]{1,0:T(8,128)(2,1)S(1)}, u32[]{:S(2)}, u32[]{:S(2)}) collective-permute-start(bf16[1600,128]{1,0:T(8,128)(2,1)S(1)} %collective-permute-done.1.refs_4_), channel_id=1, source_target_pairs={{0,704},{8,712},{16,720},{24,728},{32,736},{40,744},{48,752},{56,7... | collective-permute-start | bytes 1228808 | tf_op jit(solution)/shard_map/ppermute | solution.py:30
  55.3 3.3 %collective-permute-done.7.refs_5_ = bf16[1600,128]{1,0:T(8,128)(2,1)S(1)} collective-permute-done((bf16[1600,128]{1,0:T(8,128)(2,1)S(1)}, bf16[1600,128]{1,0:T(8,128)(2,1)S(1)}, u32[]{:S(2)}, u32[]{:S(2)}) %collective-permute-start.7) | collective-permute-done | bytes 409632 | tf_op jit(solution)/shard_map/ppermute | solution.py:30
  58.6 1.9 %collective-permute-start.8 = (bf16[1600,128]{1,0:T(8,128)(2,1)S(1)}, bf16[1600,128]{1,0:T(8,128)(2,1)S(1)}, u32[]{:S(2)}, u32[]{:S(2)}) collective-permute-start(bf16[1600,128]{1,0:T(8,128)(2,1)S(1)} %collective-permute-done.7.refs_5_), channel_id=1, source_target_pairs={{0,64},{8,72},{16,80},{24,88},{32,96},{40,104},{48,112},{56,120},{... | collective-permute-start | bytes 1228808 | tf_op jit(solution)/shard_map/ppermute | solution.py:30
  60.5 4.6 %collective-permute-start.3 = (bf16[1600,128]{1,0:T(8,128)(2,1)S(1)}, bf16[1600,128]{1,0:T(8,128)(2,1)S(1)}, u32[]{:S(2)}, u32[]{:S(2)}) collective-permute-start(bf16[1600,128]{1,0:T(8,128)(2,1)S(1)} %collective-permute-done.2.refs_6_), channel_id=1, source_target_pairs={{0,704},{8,712},{16,720},{24,728},{32,736},{40,744},{48,752},{56,7... | collective-permute-start | bytes 1228808 | tf_op jit(solution)/shard_map/ppermute | solution.py:30
  65.2 7.6 %collective-permute-start.11 = (bf16[8000,128]{1,0:T(8,128)(2,1)S(1)}, bf16[8000,128]{1,0:T(8,128)(2,1)S(1)}, u32[]{:S(2)}, u32[]{:S(2)}) collective-permute-start(bf16[8000,128]{1,0:T(8,128)(2,1)S(1)} %constant_dynamic-update-slice_fusion), channel_id=1, source_target_pairs={{0,8},{8,0},{16,24},{24,16},{32,40},{40,32},{48,56},{56,48},{64,72... | collective-permute-start | bytes 6144008 | tf_op jit(solution)/shard_map/ppermute | solution.py:30
  72.8 1.9 %collective-permute-start.9 = (bf16[1600,128]{1,0:T(8,128)(2,1)S(1)}, bf16[1600,128]{1,0:T(8,128)(2,1)S(1)}, u32[]{:S(2)}, u32[]{:S(2)}) collective-permute-start(bf16[1600,128]{1,0:T(8,128)(2,1)S(1)} %collective-permute-done.8.refs_7_), channel_id=1, source_target_pairs={{0,64},{8,72},{16,80},{24,88},{32,96},{40,104},{48,112},{56,120},{... | collective-permute-start | bytes 1228808 | tf_op jit(solution)/shard_map/ppermute | solution.py:30
  74.8 4.6 %collective-permute-start.4 = (bf16[1600,128]{1,0:T(8,128)(2,1)S(1)}, bf16[1600,128]{1,0:T(8,128)(2,1)S(1)}, u32[]{:S(2)}, u32[]{:S(2)}) collective-permute-start(bf16[1600,128]{1,0:T(8,128)(2,1)S(1)} %collective-permute-done.3.refs_8_), channel_id=1, source_target_pairs={{0,704},{8,712},{16,720},{24,728},{32,736},{40,744},{48,752},{56,7... | collective-permute-start | bytes 1228808 | tf_op jit(solution)/shard_map/ppermute | solution.py:30
  79.4 0.1 pad_maximum_fusion
  79.5 4.5 %collective-permute-start.12 = (bf16[6400,128]{1,0:T(8,128)(2,1)S(1)}, bf16[6400,128]{1,0:T(8,128)(2,1)S(1)}, u32[]{:S(2)}, u32[]{:S(2)}) collective-permute-start(bf16[6400,128]{1,0:T(8,128)(2,1)S(1)} %pad_maximum_fusion), channel_id=1, source_target_pairs={{0,8},{8,0},{16,24},{24,16},{32,40},{40,32},{48,56},{56,48},{64,72... | collective-permute-start | bytes 4915208 | tf_op jit(solution)/shard_map/ppermute | solution.py:30
  84.0 1.0 collective-permute-done.9.second
  85.0 0.9 collective-permute-done.4.first
  85.9 0.2 shard_map.78
  86.2 5.0 %collective-permute-start.13 = (bf16[3200,128]{1,0:T(8,128)(2,1)S(1)}, bf16[3200,128]{1,0:T(8,128)(2,1)S(1)}, u32[]{:S(2)}, u32[]{:S(2)}) collective-permute-start(bf16[3200,128]{1,0:T(8,128)(2,1)S(1)} %pad_maximum_fusion.1), channel_id=1, source_target_pairs={{0,8},{8,0},{16,24},{24,16},{32,40},{40,32},{48,56},{56,48},{64,72... | collective-permute-start | bytes 2457608 | tf_op jit(solution)/shard_map/ppermute | solution.py:30
  91.2 5.5 %collective-permute-start.10 = (bf16[1600,128]{1,0:T(8,128)(2,1)S(1)}, bf16[1600,128]{1,0:T(8,128)(2,1)S(1)}, u32[]{:S(2)}, u32[]{:S(2)}) collective-permute-start(bf16[1600,128]{1,0:T(8,128)(2,1)S(1)} %get-tuple-element.10), channel_id=1, source_target_pairs={{0,64},{8,712},{16,80},{24,728},{32,96},{40,744},{48,112},{56,760}... | collective-permute-start | bytes 1228808 | tf_op jit(solution)/shard_map/ppermute | solution.py:30
  96.7 5.2 %shard_map.79 = (bf16[14,3584,128]{2,1,0:T(8,128)(2,1)S(1)}, f32[14,128,128]{2,1,0:T(8,128)S(1)}, f32[8,128]{1,0:T(8,128)S(1)}) custom-call(bf16[1600,128]{1,0:T(8,128)(2,1)S(1)} %all_gather.3.refs_0_, bf16[1600,128]{1,0:T(8,128)(2,1)S(1)} %collective-permute-done.5.refs_1_, bf16[1600,128]{1,0:T(8,128)(2,1)S(1)} %collective-permute-done.refs_2_, ...), custom_call_target="tpu_custom_call" | custom-call | flops 1644167168 | bytes 34701312 | tf_op jit(solution)/shard_map/pallas_call | solution.py:204
  102.0 2.8 %collective-permute-start.14 = (bf16[1600,128]{1,0:T(8,128)(2,1)S(1)}, bf16[1600,128]{1,0:T(8,128)(2,1)S(1)}, u32[]{:S(2)}, u32[]{:S(2)}) collective-permute-start(bf16[1600,128]{1,0:T(8,128)(2,1)S(1)} %shard_map.80.refs_0_), channel_id=1, source_target_pairs={{0,8},{8,0},{16,24},{24,16},{32,40},{40,32},{48,56},{56,48},{64,72... | collective-permute-start | bytes 1228808 | tf_op jit(solution)/shard_map/ppermute | solution.py:30
  104.8 1.4 collective-permute-done.14.refs_1_
  106.2 4.8 %shard_map.81 = (bf16[128,1792]{1,0:T(8,128)(2,1)}, bf16[8,448,128]{2,1,0:T(8,128)(2,1)S(1)}, bf16[14,3584,128]{2,1,0:T(8,128)(2,1)S(1)}) custom-call(bf16[1600,128]{1,0:T(8,128)(2,1)S(1)} %shard_map.80.refs_0_, bf16[1600,128]{1,0:T(8,128)(2,1)S(1)} %collective-permute-done.14.refs_1_, ...), custom_call_target="tpu_custom_call", output_to_operand_aliasing={{2}: (5, {})} | custom-call | flops 1644167168 | bytes 13664256 | tf_op jit(solution)/shard_map/pallas_call | solution.py:232
  111.0 31.8 %all_to_all.5 = bf16[8,448,128]{2,1,0:T(8,128)(2,1)S(1)} all-to-all(bf16[8,448,128]{2,1,0:T(8,128)(2,1)S(1)} %get-tuple-element.17), channel_id=1, replica_groups=mesh['fsdp'=96,'tp'=8] {'tp'}, dimensions={0} | all-to-all | bytes 1835008 | tf_op jit(solution)/shard_map/all_to_all | solution.py:328
  142.7 0.8 reduce_sum.12
  (23 shorter events, 0.4 us)
Async XLA Ops:
  1.3 0.9 copy-start.2
  2.2 0.7 copy-start.3
  2.8 0.7 copy-start.4
  14.9 22.8 %collective-permute-start.5 = (bf16[1600,128]{1,0:T(8,128)(2,1)S(1)}, bf16[1600,128]{1,0:T(8,128)(2,1)S(1)}, u32[]{:S(2)}, u32[]{:S(2)}) collective-permute-start(bf16[1600,128]{1,0:T(8,128)(2,1)S(1)} %all_gather.3.refs_0_), channel_id=1, source_target_pairs={{0,64},{8,72},{16,80},{24,88},{32,96},{40,104},{48,112},{56,120},{... | collective-permute-start | bytes 1228808 | tf_op jit(solution)/shard_map/ppermute | solution.py:30
  20.1 19.5 %collective-permute-start = (bf16[1600,128]{1,0:T(8,128)(2,1)S(1)}, bf16[1600,128]{1,0:T(8,128)(2,1)S(1)}, u32[]{:S(2)}, u32[]{:S(2)}) collective-permute-start(bf16[1600,128]{1,0:T(8,128)(2,1)S(1)} %all_gather.3.refs_0_), channel_id=1, source_target_pairs={{0,704},{8,712},{16,720},{24,728},{32,736},{40,744},{48,752},{56,7... | collective-permute-start | bytes 1228808 | tf_op jit(solution)/shard_map/ppermute | solution.py:30
  37.7 11.0 %collective-permute-start.6 = (bf16[1600,128]{1,0:T(8,128)(2,1)S(1)}, bf16[1600,128]{1,0:T(8,128)(2,1)S(1)}, u32[]{:S(2)}, u32[]{:S(2)}) collective-permute-start(bf16[1600,128]{1,0:T(8,128)(2,1)S(1)} %collective-permute-done.5.refs_1_), channel_id=1, source_target_pairs={{0,64},{8,72},{16,80},{24,88},{32,96},{40,104},{48,112},{56,120},{... | collective-permute-start | bytes 1228808 | tf_op jit(solution)/shard_map/ppermute | solution.py:30
  39.6 11.0 %collective-permute-start.1 = (bf16[1600,128]{1,0:T(8,128)(2,1)S(1)}, bf16[1600,128]{1,0:T(8,128)(2,1)S(1)}, u32[]{:S(2)}, u32[]{:S(2)}) collective-permute-start(bf16[1600,128]{1,0:T(8,128)(2,1)S(1)} %collective-permute-done.refs_2_), channel_id=1, source_target_pairs={{0,704},{8,712},{16,720},{24,728},{32,736},{40,744},{48,752},{56,7... | collective-permute-start | bytes 1228808 | tf_op jit(solution)/shard_map/ppermute | solution.py:30
  48.7 9.9 %collective-permute-start.7 = (bf16[1600,128]{1,0:T(8,128)(2,1)S(1)}, bf16[1600,128]{1,0:T(8,128)(2,1)S(1)}, u32[]{:S(2)}, u32[]{:S(2)}) collective-permute-start(bf16[1600,128]{1,0:T(8,128)(2,1)S(1)} %collective-permute-done.6.refs_3_), channel_id=1, source_target_pairs={{0,64},{8,72},{16,80},{24,88},{32,96},{40,104},{48,112},{56,120},{... | collective-permute-start | bytes 1228808 | tf_op jit(solution)/shard_map/ppermute | solution.py:30
  50.6 9.9 %collective-permute-start.2 = (bf16[1600,128]{1,0:T(8,128)(2,1)S(1)}, bf16[1600,128]{1,0:T(8,128)(2,1)S(1)}, u32[]{:S(2)}, u32[]{:S(2)}) collective-permute-start(bf16[1600,128]{1,0:T(8,128)(2,1)S(1)} %collective-permute-done.1.refs_4_), channel_id=1, source_target_pairs={{0,704},{8,712},{16,720},{24,728},{32,736},{40,744},{48,752},{56,7... | collective-permute-start | bytes 1228808 | tf_op jit(solution)/shard_map/ppermute | solution.py:30
  58.6 14.3 %collective-permute-start.8 = (bf16[1600,128]{1,0:T(8,128)(2,1)S(1)}, bf16[1600,128]{1,0:T(8,128)(2,1)S(1)}, u32[]{:S(2)}, u32[]{:S(2)}) collective-permute-start(bf16[1600,128]{1,0:T(8,128)(2,1)S(1)} %collective-permute-done.7.refs_5_), channel_id=1, source_target_pairs={{0,64},{8,72},{16,80},{24,88},{32,96},{40,104},{48,112},{56,120},{... | collective-permute-start | bytes 1228808 | tf_op jit(solution)/shard_map/ppermute | solution.py:30
  60.5 14.3 %collective-permute-start.3 = (bf16[1600,128]{1,0:T(8,128)(2,1)S(1)}, bf16[1600,128]{1,0:T(8,128)(2,1)S(1)}, u32[]{:S(2)}, u32[]{:S(2)}) collective-permute-start(bf16[1600,128]{1,0:T(8,128)(2,1)S(1)} %collective-permute-done.2.refs_6_), channel_id=1, source_target_pairs={{0,704},{8,712},{16,720},{24,728},{32,736},{40,744},{48,752},{56,7... | collective-permute-start | bytes 1228808 | tf_op jit(solution)/shard_map/ppermute | solution.py:30
  65.2 31.5 %collective-permute-start.11 = (bf16[8000,128]{1,0:T(8,128)(2,1)S(1)}, bf16[8000,128]{1,0:T(8,128)(2,1)S(1)}, u32[]{:S(2)}, u32[]{:S(2)}) collective-permute-start(bf16[8000,128]{1,0:T(8,128)(2,1)S(1)} %constant_dynamic-update-slice_fusion), channel_id=1, source_target_pairs={{0,8},{8,0},{16,24},{24,16},{32,40},{40,32},{48,56},{56,48},{64,72... | collective-permute-start | bytes 6144008 | tf_op jit(solution)/shard_map/ppermute | solution.py:30
  72.8 12.1 %collective-permute-start.9 = (bf16[1600,128]{1,0:T(8,128)(2,1)S(1)}, bf16[1600,128]{1,0:T(8,128)(2,1)S(1)}, u32[]{:S(2)}, u32[]{:S(2)}) collective-permute-start(bf16[1600,128]{1,0:T(8,128)(2,1)S(1)} %collective-permute-done.8.refs_7_), channel_id=1, source_target_pairs={{0,64},{8,72},{16,80},{24,88},{32,96},{40,104},{48,112},{56,120},{... | collective-permute-start | bytes 1228808 | tf_op jit(solution)/shard_map/ppermute | solution.py:30
  74.8 11.1 %collective-permute-start.4 = (bf16[1600,128]{1,0:T(8,128)(2,1)S(1)}, bf16[1600,128]{1,0:T(8,128)(2,1)S(1)}, u32[]{:S(2)}, u32[]{:S(2)}) collective-permute-start(bf16[1600,128]{1,0:T(8,128)(2,1)S(1)} %collective-permute-done.3.refs_8_), channel_id=1, source_target_pairs={{0,704},{8,712},{16,720},{24,728},{32,736},{40,744},{48,752},{56,7... | collective-permute-start | bytes 1228808 | tf_op jit(solution)/shard_map/ppermute | solution.py:30
  79.5 17.2 %copy-start = (bf16[128,3584]{1,0:T(8,128)(2,1)S(1)}, bf16[128,3584]{1,0:T(8,128)(2,1)}, u32[]{:S(2)}) copy-start(bf16[128,3584]{1,0:T(8,128)(2,1)} %refs_2_.1) | copy-start | bytes 2752516
  79.5 17.2 %collective-permute-start.12 = (bf16[6400,128]{1,0:T(8,128)(2,1)S(1)}, bf16[6400,128]{1,0:T(8,128)(2,1)S(1)}, u32[]{:S(2)}, u32[]{:S(2)}) collective-permute-start(bf16[6400,128]{1,0:T(8,128)(2,1)S(1)} %pad_maximum_fusion), channel_id=1, source_target_pairs={{0,8},{8,0},{16,24},{24,16},{32,40},{40,32},{48,56},{56,48},{64,72... | collective-permute-start | bytes 4915208 | tf_op jit(solution)/shard_map/ppermute | solution.py:30
  86.2 10.5 %collective-permute-start.13 = (bf16[3200,128]{1,0:T(8,128)(2,1)S(1)}, bf16[3200,128]{1,0:T(8,128)(2,1)S(1)}, u32[]{:S(2)}, u32[]{:S(2)}) collective-permute-start(bf16[3200,128]{1,0:T(8,128)(2,1)S(1)} %pad_maximum_fusion.1), channel_id=1, source_target_pairs={{0,8},{8,0},{16,24},{24,16},{32,40},{40,32},{48,56},{56,48},{64,72... | collective-permute-start | bytes 2457608 | tf_op jit(solution)/shard_map/ppermute | solution.py:30
  91.2 14.9 %copy-start.1 = (bf16[128,1792]{1,0:T(8,128)(2,1)S(1)}, bf16[128,1792]{1,0:T(8,128)(2,1)}, u32[]{:S(2)}) copy-start(bf16[128,1792]{1,0:T(8,128)(2,1)} %refs_3_.1) | copy-start | bytes 1376260
  91.2 10.7 %collective-permute-start.10 = (bf16[1600,128]{1,0:T(8,128)(2,1)S(1)}, bf16[1600,128]{1,0:T(8,128)(2,1)S(1)}, u32[]{:S(2)}, u32[]{:S(2)}) collective-permute-start(bf16[1600,128]{1,0:T(8,128)(2,1)S(1)} %get-tuple-element.10), channel_id=1, source_target_pairs={{0,64},{8,712},{16,80},{24,728},{32,96},{40,744},{48,112},{56,760}... | collective-permute-start | bytes 1228808 | tf_op jit(solution)/shard_map/ppermute | solution.py:30
  102.0 4.2 %collective-permute-start.14 = (bf16[1600,128]{1,0:T(8,128)(2,1)S(1)}, bf16[1600,128]{1,0:T(8,128)(2,1)S(1)}, u32[]{:S(2)}, u32[]{:S(2)}) collective-permute-start(bf16[1600,128]{1,0:T(8,128)(2,1)S(1)} %shard_map.80.refs_0_), channel_id=1, source_target_pairs={{0,8},{8,0},{16,24},{24,16},{32,40},{40,32},{48,56},{56,48},{64,72... | collective-permute-start | bytes 1228808 | tf_op jit(solution)/shard_map/ppermute | solution.py:30

commit v5 on v4

--- a/solution.py
+++ b/solution.py
@@ -56,7 +56,14 @@
     return (activated, derivative)
 
 
-def pack_kernel(blocks, rows, cols, counts, out):
+def pack_kernel(*refs):
+    out, sems = refs[4], refs[9]
+    copies = [pltpu.make_async_copy(refs[i], refs[5 + i], sems.at[i]) for i in range(4)]
+    for copy in copies:
+        copy.start()
+    for copy in copies:
+        copy.wait()
+    blocks, rows, cols, counts = refs[5:9]
     owner = lax.axis_index("fsdp")
     for s in range(CAP):
         here = slice(s * BLK, (s + 1) * BLK)
@@ -80,13 +87,24 @@
 
 
 def pack(w_blocks, blk_rows, blk_cols, counts):
+    args = [
+        pltpu.with_memory_space_constraint(a, pltpu.HBM)
+        for a in (w_blocks, blk_rows, blk_cols)
+    ]
     return pl.pallas_call(
         pack_kernel,
         out_shape=jax.ShapeDtypeStruct((UNIT, BLK), jnp.bfloat16),
-        in_specs=specs(pltpu.VMEM, pltpu.SMEM, pltpu.SMEM, pltpu.SMEM),
+        in_specs=specs(pltpu.HBM, pltpu.HBM, pltpu.HBM, pl.ANY),
         out_specs=pl.BlockSpec(memory_space=pltpu.VMEM),
-        compiler_params=pltpu.CompilerParams(vmem_limit_bytes=4 * 1024 * 1024),
-    )(w_blocks, blk_rows, blk_cols, counts)
+        scratch_shapes=[
+            pltpu.VMEM(w_blocks.shape, w_blocks.dtype),
+            pltpu.SMEM(blk_rows.shape, jnp.int32),
+            pltpu.SMEM(blk_cols.shape, jnp.int32),
+            pltpu.SMEM(counts.shape, jnp.int32),
+            pltpu.SemaphoreType.DMA((4,)),
+        ],
+        compiler_params=pltpu.CompilerParams(vmem_limit_bytes=8 * 1024 * 1024),
+    )(*args, counts)
 
 
 def read_places(sources, table, places, sem):

time: 144 us -> 142 us (0.986)
  local copies, waits for them, and re-layouts: 2.46 us -> 0.26 us
    unnamed x14 -> x8, local copies, waits for them, and re-layouts: 2.4 us -> 0.21 us
where the time goes in v5:
time: 142 us
  starting transfers between devices  68.7 us (48%)
  blocking collectives  42.5 us (30%)
  waiting for transfers between devices  16.3 us (11%)
  Pallas kernels  11.3 us (8%)
  between operations  1.59 us (1%)
    ppermute x15, starting transfers between devices, shift(): return lax.ppermute(value, 'fsdp', pairs)  68.7 us
    all_to_all x1, blocking collectives, per_device(): lax.all_to_all(pieces, 'tp', split_axis=0, concat_axis=0, tiled=True)  31.7 us
    ppermute x15, waiting for transfers between devices, shift(): return lax.ppermute(value, 'fsdp', pairs)  16.3 us
    all_gather x1, blocking collectives, per_device(): lax.all_gather(mine, 'fsdp', axis=0, tiled=True, axis_index_groups=by_x)  10.8 us
    pallas_call x1, Pallas kernels, near(): pl.pallas_call(lambda *refs: near_kernel(moves, *refs), out_shape=(pltpu....  5.2 us
    pallas_call x1, Pallas kernels, far(): pl.pallas_call(lambda *refs: far_kernel(moves, *refs), out_shape=(jax.Sha...  4.81 us
  transfers between devices with their start and end apart: 15, of which 6 were waited for; matrix products, arithmetic and copies ran while one was open for 0% of the time, Pallas kernels for 4%

profile of v5, /device:TPU:1, one launch (start us, length us, event | category | flops | bytes accessed | tf_op | source)
XLA Modules:
  0.0 141.6 jit_solution(7663402915710492533)
XLA Ops:
  1.3 1.0 shard_map.77
  2.3 10.8 %all_gather.3.refs_0_ = bf16[1600,128]{1,0:T(8,128)(2,1)S(1)} all-gather(bf16[400,128]{1,0:T(8,128)(2,1)S(1)} %shard_map.77), channel_id=1, replica_groups={{0,16,32,48},{8,24,40,56},{64,80,96,112},{72,88,104,120},{128,144,160,1..., dimensions={0}, use_global_device_ids=true | all-gather | bytes 512000 | tf_op jit(solution)/shard_map/all_gather | solution.py:320
  13.2 5.1 %collective-permute-start.5 = (bf16[1600,128]{1,0:T(8,128)(2,1)S(1)}, bf16[1600,128]{1,0:T(8,128)(2,1)S(1)}, u32[]{:S(2)}, u32[]{:S(2)}) collective-permute-start(bf16[1600,128]{1,0:T(8,128)(2,1)S(1)} %all_gather.3.refs_0_), channel_id=1, source_target_pairs={{0,64},{8,72},{16,80},{24,88},{32,96},{40,104},{48,112},{56,120},{... | collective-permute-start | bytes 1228808 | tf_op jit(solution)/shard_map/ppermute | solution.py:30
  18.3 12.2 %collective-permute-start = (bf16[1600,128]{1,0:T(8,128)(2,1)S(1)}, bf16[1600,128]{1,0:T(8,128)(2,1)S(1)}, u32[]{:S(2)}, u32[]{:S(2)}) collective-permute-start(bf16[1600,128]{1,0:T(8,128)(2,1)S(1)} %all_gather.3.refs_0_), channel_id=1, source_target_pairs={{0,704},{8,712},{16,720},{24,728},{32,736},{40,744},{48,752},{56,7... | collective-permute-start | bytes 1228808 | tf_op jit(solution)/shard_map/ppermute | solution.py:30
  30.5 5.4 %collective-permute-done.5.refs_1_ = bf16[1600,128]{1,0:T(8,128)(2,1)S(1)} collective-permute-done((bf16[1600,128]{1,0:T(8,128)(2,1)S(1)}, bf16[1600,128]{1,0:T(8,128)(2,1)S(1)}, u32[]{:S(2)}, u32[]{:S(2)}) %collective-permute-start.5) | collective-permute-done | bytes 409632 | tf_op jit(solution)/shard_map/ppermute | solution.py:30
  35.9 1.9 %collective-permute-start.6 = (bf16[1600,128]{1,0:T(8,128)(2,1)S(1)}, bf16[1600,128]{1,0:T(8,128)(2,1)S(1)}, u32[]{:S(2)}, u32[]{:S(2)}) collective-permute-start(bf16[1600,128]{1,0:T(8,128)(2,1)S(1)} %collective-permute-done.5.refs_1_), channel_id=1, source_target_pairs={{0,64},{8,72},{16,80},{24,88},{32,96},{40,104},{48,112},{56,120},{... | collective-permute-start | bytes 1228808 | tf_op jit(solution)/shard_map/ppermute | solution.py:30
  37.8 4.6 %collective-permute-start.1 = (bf16[1600,128]{1,0:T(8,128)(2,1)S(1)}, bf16[1600,128]{1,0:T(8,128)(2,1)S(1)}, u32[]{:S(2)}, u32[]{:S(2)}) collective-permute-start(bf16[1600,128]{1,0:T(8,128)(2,1)S(1)} %collective-permute-done.refs_2_), channel_id=1, source_target_pairs={{0,704},{8,712},{16,720},{24,728},{32,736},{40,744},{48,752},{56,7... | collective-permute-start | bytes 1228808 | tf_op jit(solution)/shard_map/ppermute | solution.py:30
  42.4 4.4 %collective-permute-done.6.refs_3_ = bf16[1600,128]{1,0:T(8,128)(2,1)S(1)} collective-permute-done((bf16[1600,128]{1,0:T(8,128)(2,1)S(1)}, bf16[1600,128]{1,0:T(8,128)(2,1)S(1)}, u32[]{:S(2)}, u32[]{:S(2)}) %collective-permute-start.6) | collective-permute-done | bytes 409632 | tf_op jit(solution)/shard_map/ppermute | solution.py:30
  46.8 1.9 %collective-permute-start.7 = (bf16[1600,128]{1,0:T(8,128)(2,1)S(1)}, bf16[1600,128]{1,0:T(8,128)(2,1)S(1)}, u32[]{:S(2)}, u32[]{:S(2)}) collective-permute-start(bf16[1600,128]{1,0:T(8,128)(2,1)S(1)} %collective-permute-done.6.refs_3_), channel_id=1, source_target_pairs={{0,64},{8,72},{16,80},{24,88},{32,96},{40,104},{48,112},{56,120},{... | collective-permute-start | bytes 1228808 | tf_op jit(solution)/shard_map/ppermute | solution.py:30
  48.8 4.6 %collective-permute-start.2 = (bf16[1600,128]{1,0:T(8,128)(2,1)S(1)}, bf16[1600,128]{1,0:T(8,128)(2,1)S(1)}, u32[]{:S(2)}, u32[]{:S(2)}) collective-permute-start(bf16[1600,128]{1,0:T(8,128)(2,1)S(1)} %collective-permute-done.1.refs_4_), channel_id=1, source_target_pairs={{0,704},{8,712},{16,720},{24,728},{32,736},{40,744},{48,752},{56,7... | collective-permute-start | bytes 1228808 | tf_op jit(solution)/shard_map/ppermute | solution.py:30
  53.3 0.1 constant_dynamic-update-slice_fusion.3
  53.4 0.1 constant_dynamic-update-slice_fusion.2
  53.5 3.3 %collective-permute-done.7.refs_5_ = bf16[1600,128]{1,0:T(8,128)(2,1)S(1)} collective-permute-done((bf16[1600,128]{1,0:T(8,128)(2,1)S(1)}, bf16[1600,128]{1,0:T(8,128)(2,1)S(1)}, u32[]{:S(2)}, u32[]{:S(2)}) %collective-permute-start.7) | collective-permute-done | bytes 409632 | tf_op jit(solution)/shard_map/ppermute | solution.py:30
  56.7 1.9 %collective-permute-start.8 = (bf16[1600,128]{1,0:T(8,128)(2,1)S(1)}, bf16[1600,128]{1,0:T(8,128)(2,1)S(1)}, u32[]{:S(2)}, u32[]{:S(2)}) collective-permute-start(bf16[1600,128]{1,0:T(8,128)(2,1)S(1)} %collective-permute-done.7.refs_5_), channel_id=1, source_target_pairs={{0,64},{8,72},{16,80},{24,88},{32,96},{40,104},{48,112},{56,120},{... | collective-permute-start | bytes 1228808 | tf_op jit(solution)/shard_map/ppermute | solution.py:30
  58.7 4.6 %collective-permute-start.3 = (bf16[1600,128]{1,0:T(8,128)(2,1)S(1)}, bf16[1600,128]{1,0:T(8,128)(2,1)S(1)}, u32[]{:S(2)}, u32[]{:S(2)}) collective-permute-start(bf16[1600,128]{1,0:T(8,128)(2,1)S(1)} %collective-permute-done.2.refs_6_), channel_id=1, source_target_pairs={{0,704},{8,712},{16,720},{24,728},{32,736},{40,744},{48,752},{56,7... | collective-permute-start | bytes 1228808 | tf_op jit(solution)/shard_map/ppermute | solution.py:30
  63.2 0.1 constant_dynamic-update-slice_fusion.1
  63.4 7.6 %collective-permute-start.11 = (bf16[8000,128]{1,0:T(8,128)(2,1)S(1)}, bf16[8000,128]{1,0:T(8,128)(2,1)S(1)}, u32[]{:S(2)}, u32[]{:S(2)}) collective-permute-start(bf16[8000,128]{1,0:T(8,128)(2,1)S(1)} %constant_dynamic-update-slice_fusion), channel_id=1, source_target_pairs={{0,8},{8,0},{16,24},{24,16},{32,40},{40,32},{48,56},{56,48},{64,72... | collective-permute-start | bytes 6144008 | tf_op jit(solution)/shard_map/ppermute | solution.py:30
  71.0 1.9 %collective-permute-start.9 = (bf16[1600,128]{1,0:T(8,128)(2,1)S(1)}, bf16[1600,128]{1,0:T(8,128)(2,1)S(1)}, u32[]{:S(2)}, u32[]{:S(2)}) collective-permute-start(bf16[1600,128]{1,0:T(8,128)(2,1)S(1)} %collective-permute-done.8.refs_7_), channel_id=1, source_target_pairs={{0,64},{8,72},{16,80},{24,88},{32,96},{40,104},{48,112},{56,120},{... | collective-permute-start | bytes 1228808 | tf_op jit(solution)/shard_map/ppermute | solution.py:30
  73.0 4.6 %collective-permute-start.4 = (bf16[1600,128]{1,0:T(8,128)(2,1)S(1)}, bf16[1600,128]{1,0:T(8,128)(2,1)S(1)}, u32[]{:S(2)}, u32[]{:S(2)}) collective-permute-start(bf16[1600,128]{1,0:T(8,128)(2,1)S(1)} %collective-permute-done.3.refs_8_), channel_id=1, source_target_pairs={{0,704},{8,712},{16,720},{24,728},{32,736},{40,744},{48,752},{56,7... | collective-permute-start | bytes 1228808 | tf_op jit(solution)/shard_map/ppermute | solution.py:30
  77.5 0.1 pad_maximum_fusion
  77.7 4.5 %collective-permute-start.12 = (bf16[6400,128]{1,0:T(8,128)(2,1)S(1)}, bf16[6400,128]{1,0:T(8,128)(2,1)S(1)}, u32[]{:S(2)}, u32[]{:S(2)}) collective-permute-start(bf16[6400,128]{1,0:T(8,128)(2,1)S(1)} %pad_maximum_fusion), channel_id=1, source_target_pairs={{0,8},{8,0},{16,24},{24,16},{32,40},{40,32},{48,56},{56,48},{64,72... | collective-permute-start | bytes 4915208 | tf_op jit(solution)/shard_map/ppermute | solution.py:30
  82.2 1.0 collective-permute-done.9.second
  83.2 0.9 collective-permute-done.4.first
  84.1 0.2 shard_map.78
  84.4 5.0 %collective-permute-start.13 = (bf16[3200,128]{1,0:T(8,128)(2,1)S(1)}, bf16[3200,128]{1,0:T(8,128)(2,1)S(1)}, u32[]{:S(2)}, u32[]{:S(2)}) collective-permute-start(bf16[3200,128]{1,0:T(8,128)(2,1)S(1)} %pad_maximum_fusion.1), channel_id=1, source_target_pairs={{0,8},{8,0},{16,24},{24,16},{32,40},{40,32},{48,56},{56,48},{64,72... | collective-permute-start | bytes 2457608 | tf_op jit(solution)/shard_map/ppermute | solution.py:30
  89.4 5.5 %collective-permute-start.10 = (bf16[1600,128]{1,0:T(8,128)(2,1)S(1)}, bf16[1600,128]{1,0:T(8,128)(2,1)S(1)}, u32[]{:S(2)}, u32[]{:S(2)}) collective-permute-start(bf16[1600,128]{1,0:T(8,128)(2,1)S(1)} %get-tuple-element.10), channel_id=1, source_target_pairs={{0,64},{8,712},{16,80},{24,728},{32,96},{40,744},{48,112},{56,760}... | collective-permute-start | bytes 1228808 | tf_op jit(solution)/shard_map/ppermute | solution.py:30
  94.9 5.2 %shard_map.79 = (bf16[14,3584,128]{2,1,0:T(8,128)(2,1)S(1)}, f32[14,128,128]{2,1,0:T(8,128)S(1)}, f32[8,128]{1,0:T(8,128)S(1)}) custom-call(bf16[1600,128]{1,0:T(8,128)(2,1)S(1)} %all_gather.3.refs_0_, bf16[1600,128]{1,0:T(8,128)(2,1)S(1)} %collective-permute-done.5.refs_1_, bf16[1600,128]{1,0:T(8,128)(2,1)S(1)} %collective-permute-done.refs_2_, ...), custom_call_target="tpu_custom_call" | custom-call | flops 1644167168 | bytes 34701312 | tf_op jit(solution)/shard_map/pallas_call | solution.py:222
  100.1 2.8 %collective-permute-start.14 = (bf16[1600,128]{1,0:T(8,128)(2,1)S(1)}, bf16[1600,128]{1,0:T(8,128)(2,1)S(1)}, u32[]{:S(2)}, u32[]{:S(2)}) collective-permute-start(bf16[1600,128]{1,0:T(8,128)(2,1)S(1)} %shard_map.80.refs_0_), channel_id=1, source_target_pairs={{0,8},{8,0},{16,24},{24,16},{32,40},{40,32},{48,56},{56,48},{64,72... | collective-permute-start | bytes 1228808 | tf_op jit(solution)/shard_map/ppermute | solution.py:30
  103.0 1.4 collective-permute-done.14.refs_1_
  104.3 4.8 %shard_map.81 = (bf16[128,1792]{1,0:T(8,128)(2,1)}, bf16[8,448,128]{2,1,0:T(8,128)(2,1)S(1)}, bf16[14,3584,128]{2,1,0:T(8,128)(2,1)S(1)}) custom-call(bf16[1600,128]{1,0:T(8,128)(2,1)S(1)} %shard_map.80.refs_0_, bf16[1600,128]{1,0:T(8,128)(2,1)S(1)} %collective-permute-done.14.refs_1_, ...), custom_call_target="tpu_custom_call", output_to_operand_aliasing={{2}: (5, {})} | custom-call | flops 1644167168 | bytes 13664256 | tf_op jit(solution)/shard_map/pallas_call | solution.py:250
  109.2 31.7 %all_to_all.5 = bf16[8,448,128]{2,1,0:T(8,128)(2,1)S(1)} all-to-all(bf16[8,448,128]{2,1,0:T(8,128)(2,1)S(1)} %get-tuple-element.17), channel_id=1, replica_groups=mesh['fsdp'=96,'tp'=8] {'tp'}, dimensions={0} | all-to-all | bytes 1835008 | tf_op jit(solution)/shard_map/all_to_all | solution.py:346
  140.9 0.8 reduce_sum.12
  (17 shorter events, 0.2 us)
Async XLA Ops:
  13.2 22.7 %collective-permute-start.5 = (bf16[1600,128]{1,0:T(8,128)(2,1)S(1)}, bf16[1600,128]{1,0:T(8,128)(2,1)S(1)}, u32[]{:S(2)}, u32[]{:S(2)}) collective-permute-start(bf16[1600,128]{1,0:T(8,128)(2,1)S(1)} %all_gather.3.refs_0_), channel_id=1, source_target_pairs={{0,64},{8,72},{16,80},{24,88},{32,96},{40,104},{48,112},{56,120},{... | collective-permute-start | bytes 1228808 | tf_op jit(solution)/shard_map/ppermute | solution.py:30
  18.3 19.5 %collective-permute-start = (bf16[1600,128]{1,0:T(8,128)(2,1)S(1)}, bf16[1600,128]{1,0:T(8,128)(2,1)S(1)}, u32[]{:S(2)}, u32[]{:S(2)}) collective-permute-start(bf16[1600,128]{1,0:T(8,128)(2,1)S(1)} %all_gather.3.refs_0_), channel_id=1, source_target_pairs={{0,704},{8,712},{16,720},{24,728},{32,736},{40,744},{48,752},{56,7... | collective-permute-start | bytes 1228808 | tf_op jit(solution)/shard_map/ppermute | solution.py:30
  35.9 11.0 %collective-permute-start.6 = (bf16[1600,128]{1,0:T(8,128)(2,1)S(1)}, bf16[1600,128]{1,0:T(8,128)(2,1)S(1)}, u32[]{:S(2)}, u32[]{:S(2)}) collective-permute-start(bf16[1600,128]{1,0:T(8,128)(2,1)S(1)} %collective-permute-done.5.refs_1_), channel_id=1, source_target_pairs={{0,64},{8,72},{16,80},{24,88},{32,96},{40,104},{48,112},{56,120},{... | collective-permute-start | bytes 1228808 | tf_op jit(solution)/shard_map/ppermute | solution.py:30
  37.8 11.0 %collective-permute-start.1 = (bf16[1600,128]{1,0:T(8,128)(2,1)S(1)}, bf16[1600,128]{1,0:T(8,128)(2,1)S(1)}, u32[]{:S(2)}, u32[]{:S(2)}) collective-permute-start(bf16[1600,128]{1,0:T(8,128)(2,1)S(1)} %collective-permute-done.refs_2_), channel_id=1, source_target_pairs={{0,704},{8,712},{16,720},{24,728},{32,736},{40,744},{48,752},{56,7... | collective-permute-start | bytes 1228808 | tf_op jit(solution)/shard_map/ppermute | solution.py:30
  46.8 9.9 %collective-permute-start.7 = (bf16[1600,128]{1,0:T(8,128)(2,1)S(1)}, bf16[1600,128]{1,0:T(8,128)(2,1)S(1)}, u32[]{:S(2)}, u32[]{:S(2)}) collective-permute-start(bf16[1600,128]{1,0:T(8,128)(2,1)S(1)} %collective-permute-done.6.refs_3_), channel_id=1, source_target_pairs={{0,64},{8,72},{16,80},{24,88},{32,96},{40,104},{48,112},{56,120},{... | collective-permute-start | bytes 1228808 | tf_op jit(solution)/shard_map/ppermute | solution.py:30
  48.8 9.9 %collective-permute-start.2 = (bf16[1600,128]{1,0:T(8,128)(2,1)S(1)}, bf16[1600,128]{1,0:T(8,128)(2,1)S(1)}, u32[]{:S(2)}, u32[]{:S(2)}) collective-permute-start(bf16[1600,128]{1,0:T(8,128)(2,1)S(1)} %collective-permute-done.1.refs_4_), channel_id=1, source_target_pairs={{0,704},{8,712},{16,720},{24,728},{32,736},{40,744},{48,752},{56,7... | collective-permute-start | bytes 1228808 | tf_op jit(solution)/shard_map/ppermute | solution.py:30
  56.7 14.3 %collective-permute-start.8 = (bf16[1600,128]{1,0:T(8,128)(2,1)S(1)}, bf16[1600,128]{1,0:T(8,128)(2,1)S(1)}, u32[]{:S(2)}, u32[]{:S(2)}) collective-permute-start(bf16[1600,128]{1,0:T(8,128)(2,1)S(1)} %collective-permute-done.7.refs_5_), channel_id=1, source_target_pairs={{0,64},{8,72},{16,80},{24,88},{32,96},{40,104},{48,112},{56,120},{... | collective-permute-start | bytes 1228808 | tf_op jit(solution)/shard_map/ppermute | solution.py:30
  58.7 14.3 %collective-permute-start.3 = (bf16[1600,128]{1,0:T(8,128)(2,1)S(1)}, bf16[1600,128]{1,0:T(8,128)(2,1)S(1)}, u32[]{:S(2)}, u32[]{:S(2)}) collective-permute-start(bf16[1600,128]{1,0:T(8,128)(2,1)S(1)} %collective-permute-done.2.refs_6_), channel_id=1, source_target_pairs={{0,704},{8,712},{16,720},{24,728},{32,736},{40,744},{48,752},{56,7... | collective-permute-start | bytes 1228808 | tf_op jit(solution)/shard_map/ppermute | solution.py:30
  63.4 31.5 %collective-permute-start.11 = (bf16[8000,128]{1,0:T(8,128)(2,1)S(1)}, bf16[8000,128]{1,0:T(8,128)(2,1)S(1)}, u32[]{:S(2)}, u32[]{:S(2)}) collective-permute-start(bf16[8000,128]{1,0:T(8,128)(2,1)S(1)} %constant_dynamic-update-slice_fusion), channel_id=1, source_target_pairs={{0,8},{8,0},{16,24},{24,16},{32,40},{40,32},{48,56},{56,48},{64,72... | collective-permute-start | bytes 6144008 | tf_op jit(solution)/shard_map/ppermute | solution.py:30
  71.0 12.1 %collective-permute-start.9 = (bf16[1600,128]{1,0:T(8,128)(2,1)S(1)}, bf16[1600,128]{1,0:T(8,128)(2,1)S(1)}, u32[]{:S(2)}, u32[]{:S(2)}) collective-permute-start(bf16[1600,128]{1,0:T(8,128)(2,1)S(1)} %collective-permute-done.8.refs_7_), channel_id=1, source_target_pairs={{0,64},{8,72},{16,80},{24,88},{32,96},{40,104},{48,112},{56,120},{... | collective-permute-start | bytes 1228808 | tf_op jit(solution)/shard_map/ppermute | solution.py:30
  73.0 11.1 %collective-permute-start.4 = (bf16[1600,128]{1,0:T(8,128)(2,1)S(1)}, bf16[1600,128]{1,0:T(8,128)(2,1)S(1)}, u32[]{:S(2)}, u32[]{:S(2)}) collective-permute-start(bf16[1600,128]{1,0:T(8,128)(2,1)S(1)} %collective-permute-done.3.refs_8_), channel_id=1, source_target_pairs={{0,704},{8,712},{16,720},{24,728},{32,736},{40,744},{48,752},{56,7... | collective-permute-start | bytes 1228808 | tf_op jit(solution)/shard_map/ppermute | solution.py:30
  77.7 17.2 %copy-start = (bf16[128,3584]{1,0:T(8,128)(2,1)S(1)}, bf16[128,3584]{1,0:T(8,128)(2,1)}, u32[]{:S(2)}) copy-start(bf16[128,3584]{1,0:T(8,128)(2,1)} %refs_2_.3) | copy-start | bytes 2752516
  77.7 17.2 %collective-permute-start.12 = (bf16[6400,128]{1,0:T(8,128)(2,1)S(1)}, bf16[6400,128]{1,0:T(8,128)(2,1)S(1)}, u32[]{:S(2)}, u32[]{:S(2)}) collective-permute-start(bf16[6400,128]{1,0:T(8,128)(2,1)S(1)} %pad_maximum_fusion), channel_id=1, source_target_pairs={{0,8},{8,0},{16,24},{24,16},{32,40},{40,32},{48,56},{56,48},{64,72... | collective-permute-start | bytes 4915208 | tf_op jit(solution)/shard_map/ppermute | solution.py:30
  84.4 10.5 %collective-permute-start.13 = (bf16[3200,128]{1,0:T(8,128)(2,1)S(1)}, bf16[3200,128]{1,0:T(8,128)(2,1)S(1)}, u32[]{:S(2)}, u32[]{:S(2)}) collective-permute-start(bf16[3200,128]{1,0:T(8,128)(2,1)S(1)} %pad_maximum_fusion.1), channel_id=1, source_target_pairs={{0,8},{8,0},{16,24},{24,16},{32,40},{40,32},{48,56},{56,48},{64,72... | collective-permute-start | bytes 2457608 | tf_op jit(solution)/shard_map/ppermute | solution.py:30
  89.4 14.9 %copy-start.1 = (bf16[128,1792]{1,0:T(8,128)(2,1)S(1)}, bf16[128,1792]{1,0:T(8,128)(2,1)}, u32[]{:S(2)}) copy-start(bf16[128,1792]{1,0:T(8,128)(2,1)} %refs_3_.2) | copy-start | bytes 1376260
  89.4 10.7 %collective-permute-start.10 = (bf16[1600,128]{1,0:T(8,128)(2,1)S(1)}, bf16[1600,128]{1,0:T(8,128)(2,1)S(1)}, u32[]{:S(2)}, u32[]{:S(2)}) collective-permute-start(bf16[1600,128]{1,0:T(8,128)(2,1)S(1)} %get-tuple-element.10), channel_id=1, source_target_pairs={{0,64},{8,712},{16,80},{24,728},{32,96},{40,744},{48,112},{56,760}... | collective-permute-start | bytes 1228808 | tf_op jit(solution)/shard_map/ppermute | solution.py:30
  100.1 4.2 %collective-permute-start.14 = (bf16[1600,128]{1,0:T(8,128)(2,1)S(1)}, bf16[1600,128]{1,0:T(8,128)(2,1)S(1)}, u32[]{:S(2)}, u32[]{:S(2)}) collective-permute-start(bf16[1600,128]{1,0:T(8,128)(2,1)S(1)} %shard_map.80.refs_0_), channel_id=1, source_target_pairs={{0,8},{8,0},{16,24},{24,16},{32,40},{40,32},{48,56},{56,48},{64,72... | collective-permute-start | bytes 1228808 | tf_op jit(solution)/shard_map/ppermute | solution.py:30
